TPU v7x, 32 devices: a whole 2x2x4 slice. The times are simulated.
32 devices in a mesh: gx: 4 (over y, x), gy: 4 (over z), gz: 2 (over core).
Axes of the slice: x: 2, y: 2, z: 4, core: 2. Of those that a mesh axis runs over, the one named last changes fastest.
Arguments:
- conserved: float32 [14, 32, 256, 512], P(None, 'gx', 'gy', 'gz')
- char_left: float32 [14, 14], replicated
- char_right: float32 [14, 14], replicated
- shock_list: int32 [4, 4, 2, 128], P('gx', 'gy', 'gz'), may hold values from 0 to 511, as said below
- shock_count: int32 [4, 4, 2], P('gx', 'gy', 'gz'), may hold values from 32 to 128, as said below
Outputs:
- advanced: float32 [14, 32, 256, 512], P(None, 'gx', 'gy', 'gz')
Inputs may be any that keep to these rules, and one draw needn't show every extreme that they name: `shock_list`: the entries of one device's list are distinct local pencil indices; only the first shock_count of them are shocked pencils. `shock_count`: in every column of devices along gx (fixed gy and gz index) one device has 128 shocked pencils and every other device has 32, so a column holds 224 in all.
All inputs are finite; a program needn't handle non-finite values.
Results may differ from a plain program's by a relative error of at most 0.00005.
Values sent between devices are 32-bit elements; how exact they have to be, the bound alone decides.
No kernel may reach another device: no remote copies, remote signals or barrier semaphores. Data moves between devices by JAX's collectives and lax.ppermute only.
A program may use at most 192 MiB of HBM per device.

v0:
```python
import functools

import jax
import jax.numpy as jnp
from jax import lax
from jax.experimental import pallas as pl
from jax.experimental.pallas import tpu as pltpu
from jax.sharding import PartitionSpec as P

SPECIES = 9
VARIABLES = 14
WIDTH = 3
GROUP = 16
LANES = 128
LEAD = 8

gas_excess = 0.4
time_step = 0.2
weno_epsilon = 1e-06

F32 = jnp.float32
BF16 = jnp.bfloat16


def split(values):
    high = values.astype(BF16)
    low = (values - high.astype(F32)).astype(BF16)
    return high, low


def dot(left, right):
    return jnp.dot(left, right, preferred_element_type=F32)


def state_of(parts):
    density = parts[0]
    for index in range(1, SPECIES):
        density = density + parts[index]
    inverse = pl.reciprocal(density, approx=True)
    first, second, last = parts[SPECIES], parts[SPECIES + 1], parts[SPECIES + 2]
    kinetic = 0.5 * (first * first + second * second + last * last) * inverse
    pressure = gas_excess * (parts[SPECIES + 3] - parts[SPECIES + 4] - kinetic)
    return inverse, pressure


def flux_of(parts, normal):
    inverse, pressure = state_of(parts)
    velocity = parts[SPECIES + normal] * inverse
    result = [part * velocity for part in parts]
    result[SPECIES + normal] = result[SPECIES + normal] + pressure
    result[SPECIES + 3] = result[SPECIES + 3] + pressure * velocity
    return result


def pack_y_kernel(u_ref, tail_ref, head_ref, sem):
    cells_x, cells_y = u_ref.shape[1], u_ref.shape[2]
    for x in range(cells_x):
        for j in range(WIDTH):
            pltpu.make_async_copy(
                u_ref.at[:, x, pl.ds(cells_y - WIDTH + j, 1), :], tail_ref.at[j, :, pl.ds(x, 1), :], sem
            ).start()
            pltpu.make_async_copy(
                u_ref.at[:, x, pl.ds(j, 1), :], head_ref.at[j, :, pl.ds(x, 1), :], sem
            ).start()
    pltpu.make_async_copy(tail_ref, tail_ref, sem).wait()
    pltpu.make_async_copy(head_ref, head_ref, sem).wait()


def pack_y(conserved):
    cells_x, cells_z = conserved.shape[1], conserved.shape[3]
    face = jax.ShapeDtypeStruct((WIDTH, VARIABLES, cells_x, cells_z), F32)
    return pl.pallas_call(
        pack_y_kernel,
        out_shape=[face, face],
        in_specs=[pl.BlockSpec(memory_space=pl.ANY)],
        out_specs=[pl.BlockSpec(memory_space=pltpu.VMEM)] * 2,
        scratch_shapes=[pltpu.SemaphoreType.DMA(())],
        cost_estimate=pl.CostEstimate(flops=0, bytes_accessed=2_000_000, transcendentals=0),
        name="pack_y",
    )(conserved)


def pack_z_kernel(u_ref, out_ref):
    cells_z = u_ref.shape[3]
    lane = lax.broadcasted_iota(jnp.int32, (u_ref.shape[2], LANES), 1)
    packed = jnp.zeros((u_ref.shape[2], LANES), F32)
    for v in range(VARIABLES):
        both = jnp.where(lane < LANES // 2, u_ref[v, 0, :, :LANES], u_ref[v, 0, :, cells_z - LANES :])
        packed = jnp.where(lane >> 3 == v, pltpu.roll(both, 8 * v + WIDTH, 1), packed)
    out_ref[...] = packed


def pack_z(conserved):
    _, cells_x, cells_y, cells_z = conserved.shape
    return pl.pallas_call(
        pack_z_kernel,
        out_shape=jax.ShapeDtypeStruct((cells_x * cells_y, LANES), F32),
        grid=(cells_x,),
        in_specs=[pl.BlockSpec((VARIABLES, 1, cells_y, cells_z), lambda x: (0, x, 0, 0))],
        out_specs=pl.BlockSpec((cells_y, LANES), lambda x: (x, 0)),
        compiler_params=pltpu.CompilerParams(vmem_limit_bytes=16 << 20),
        cost_estimate=pl.CostEstimate(flops=4_000_000, bytes_accessed=7_600_000, transcendentals=0),
        name="pack_z",
    )(conserved)


def exchange_z(packed):
    count = lax.axis_size("gz")
    if count == 1:
        return packed
    ahead = [(i, (i + 1) % count) for i in range(count)]
    from_left = lax.ppermute(packed, "gz", ahead)
    if count == 2:
        return from_left
    from_right = lax.ppermute(packed, "gz", [(b, a) for a, b in ahead])
    lane = jnp.arange(LANES, dtype=jnp.int32)[None, :]
    return jnp.where(lane & 7 < WIDTH, from_left, from_right)


def spread_matrix(matrix, size):
    rows = VARIABLES * GROUP
    pick = lax.broadcasted_iota(jnp.int32, (rows, VARIABLES), 0) >> 4
    pick = (pick == lax.broadcasted_iota(jnp.int32, (rows, VARIABLES), 1)).astype(F32)
    tall = jnp.dot(pick, matrix, precision=lax.Precision.HIGHEST, preferred_element_type=F32)
    wide = lax.dot_general(
        tall, pick, (((1,), (1,)), ((), ())), precision=lax.Precision.HIGHEST, preferred_element_type=F32
    )
    row = lax.broadcasted_iota(jnp.int32, (rows, rows), 0) & (GROUP - 1)
    column = lax.broadcasted_iota(jnp.int32, (rows, rows), 1) & (GROUP - 1)
    return split(jnp.where(row == column, wide, 0.0))


def stencil(offset):
    size = jnp.abs(offset)
    weight = jnp.where(size == 1, 45.0, jnp.where(size == 2, -9.0, jnp.where(size == 3, 1.0, 0.0)))
    return jnp.where(offset < 0, -weight, weight)


def main_kernel(
    list_ref,
    count_ref,
    u_ref,
    face_ref,
    left_ref,
    right_ref,
    row_ref,
    out_ref,
    cells,
    pencils,
    turned,
    speed_t,
    press_t,
    g_out,
    g_in,
    delta,
    triple,
    smooth,
    curve,
    faces,
    change,
    edge,
    edge_t,
    slot_hot,
    speed_y,
    press_y,
    speed_z,
    press_z,
    flux_z,
    flux_y,
    band_y,
    band_z,
    band_h,
    picked_sem,
    in_sem,
    out_sem,
):
    _, cells_x, cells_y, cells_z = u_ref.shape
    slots = row_ref.shape[1]
    total = cells_x * cells_y
    span = turned.shape[1]
    def fetch(p, carry):
        place = list_ref[p]
        pltpu.make_async_copy(
            u_ref.at[:, place // cells_y, pl.ds(place % cells_y, 1), :], pencils.at[:, pl.ds(p, 1), :], picked_sem
        ).start()
        return carry

    lax.fori_loop(0, slots, fetch, 0)
    incoming = [
        pltpu.make_async_copy(u_ref.at[:, x], cells.at[:, pl.ds(x * cells_y, cells_y), :], in_sem.at[x])
        for x in range(cells_x)
    ]
    for copy in incoming:
        copy.start()

    left_high, left_low = spread_matrix(0.5 * left_ref[...], slots)
    right_high, right_low = spread_matrix(20.0 * right_ref[...], slots)
    live = count_ref[0]
    lane_slots = lax.broadcasted_iota(jnp.int32, (1, slots), 1)
    wanted = jnp.where(lane_slots < live, row_ref[...], -1)

    block_rows = band_y.shape[0]
    row = lax.broadcasted_iota(jnp.int32, (block_rows, block_rows), 0)
    column = lax.broadcasted_iota(jnp.int32, (block_rows, block_rows), 1)
    inside = row // cells_y == column // cells_y
    weights = jnp.where(inside, stencil(column - row), 0.0).astype(BF16)
    band_y[:, :block_rows] = weights
    band_y[:, block_rows:] = weights
    row = lax.broadcasted_iota(jnp.int32, (cells_z, cells_z), 0)
    column = lax.broadcasted_iota(jnp.int32, (cells_z, cells_z), 1)
    weights = stencil(row - column).astype(BF16)
    band_z[:cells_z, :] = weights
    band_z[cells_z:, :] = weights
    kind = lax.broadcasted_iota(jnp.int32, (LANES, cells_z), 0) & 7
    column = lax.broadcasted_iota(jnp.int32, (LANES, cells_z), 1)
    place = jnp.where(kind < WIDTH, kind - WIDTH, kind - WIDTH + cells_z)
    band_h[...] = jnp.where(kind < 2 * WIDTH, stencil(place - column), 0.0)

    for begin in range(0, total, LANES):
        edge_t[:, begin : begin + LANES] = face_ref[begin : begin + LANES, :].T
    fluxes = flux_of([edge_t[8 * v : 8 * v + 8, :] for v in range(VARIABLES)], 2)
    for v in range(VARIABLES):
        edge_t[8 * v : 8 * v + 8, :] = fluxes[v]
    for begin in range(0, total, LANES):
        pencil = begin + lax.broadcasted_iota(jnp.int32, (LANES, slots), 0)
        hot = (wanted == pencil).astype(F32)
        calm = 1.0 - jnp.sum(hot, axis=1, keepdims=True)
        hot = hot.astype(BF16)
        slot_hot[begin : begin + LANES, :slots] = hot
        slot_hot[begin : begin + LANES, slots:] = hot
        high, low = split(edge_t[:, begin : begin + LANES].T * calm)
        edge[begin : begin + LANES, :LANES] = high
        edge[begin : begin + LANES, LANES:] = low

    def neighbour(p, carry):
        speed_t[pl.ds(p, 1), :] = face_ref[pl.ds(list_ref[p], 1), :]
        return carry

    lax.fori_loop(0, slots, neighbour, 0, unroll=8)
    border = speed_t[0:slots, :].T

    pltpu.make_async_copy(pencils, pencils, picked_sem).wait()
    for v in range(VARIABLES):
        tile = border[8 * v : 8 * v + 8, :]
        turned[v, 0:LEAD, :] = tile
        turned[v, span - 8 : span, :] = tile
        turned[v, LEAD - WIDTH : LEAD - WIDTH + 8, :] = tile
        turned[v, LEAD + cells_z - WIDTH : LEAD + cells_z - WIDTH + 8, :] = tile
        for begin in range(0, cells_z, LANES):
            turned[v, LEAD + begin : LEAD + begin + LANES, :] = pencils[v, :, begin : begin + LANES].T

    top = jnp.zeros((8, slots), F32)
    for begin in range(0, span, 8):
        parts = [turned[v, begin : begin + 8, :] for v in range(VARIABLES)]
        inverse, pressure = state_of(parts)
        velocity = parts[SPECIES + 2] * inverse
        speed_t[begin : begin + 8, :] = velocity
        press_t[begin : begin + 8, :] = pressure
        size = jnp.abs(velocity)
        if begin < LEAD - WIDTH or begin + 8 > LEAD + cells_z + WIDTH:
            at = begin + lax.broadcasted_iota(jnp.int32, (8, slots), 0)
            size = jnp.where((at >= LEAD - WIDTH) & (at < LEAD + cells_z + WIDTH), size, 0.0)
        top = jnp.maximum(top, size)
    wave = 0.5 * (jnp.max(top, axis=0, keepdims=True) + 1.0)

    rows = VARIABLES * GROUP

    def project(index, carry):
        at = pl.ds(pl.multiple_of(index * GROUP, GROUP), GROUP)
        velocity = 0.5 * speed_t[at, :]
        pressure = 0.5 * press_t[at, :]
        parts = [turned[v, at, :] for v in range(VARIABLES)]
        flux = [part * velocity for part in parts]
        flux[SPECIES + 2] = flux[SPECIES + 2] + pressure
        flux[SPECIES + 3] = flux[SPECIES + 3] + 2.0 * pressure * velocity
        high, low = [], []
        for v in range(VARIABLES):
            one, two = split(jnp.concatenate([flux[v], wave * parts[v]], axis=1))
            high.append(one)
            low.append(two)
        high = jnp.concatenate(high, axis=0)
        low = jnp.concatenate(low, axis=0)
        both = dot(left_high, high) + dot(left_high, low) + dot(left_low, high)
        both = both.reshape(VARIABLES, GROUP, 2 * slots)
        g_out[:, at, :] = both[:, :, :slots] + both[:, :, slots:]
        g_in[:, at, :] = both[:, :, :slots] - both[:, :, slots:]
        return carry

    lax.fori_loop(0, span // GROUP, project, 0)

    def upwind(i, carry):
        for side, source in enumerate((g_out, g_in)):
            for begin in range(0, span, 8):
                step = source[i, begin + 1 : begin + 9, :] - source[i, begin : begin + 8, :]
                delta[side, begin : begin + 8, :] = step
                triple[side, begin : begin + 8, :] = 3.0 * step
            for begin in range(8, span, 8):
                bend = delta[side, begin : begin + 8, :] - delta[side, begin - 1 : begin + 7, :]
                curve[side, begin : begin + 8, :] = bend
                smooth[side, begin : begin + 8, :] = (13.0 / 3.0 * bend) * bend + weno_epsilon
            bend = delta[side, 1:9, :] - delta[side, 0:8, :]
            curve[side, 1:9, :] = bend
            smooth[side, 1:9, :] = (13.0 / 3.0 * bend) * bend + weno_epsilon
        for begin in range(0, cells_z + 8, 8):
            at = begin + LEAD - 1

            def read(ref, side, offset):
                return ref[side, at + offset : at + offset + 8, :]

            value = None
            for side, source, way in ((0, g_out, 1), (1, g_in, -1)):
                back = 0 if side == 0 else 1
                if side == 0:
                    d1, d2, d3, d4 = (read(delta, 0, o) for o in (-2, -1, 0, 1))
                    three2, three3 = read(triple, 0, -1), read(triple, 0, 0)
                    s1, s2, s3 = (read(smooth, 0, o) for o in (-1, 0, 1))
                    z1, z2, z3 = (read(curve, 0, o) for o in (-1, 0, 1))
                else:
                    d1, d2, d3, d4 = (read(delta, 1, o) for o in (2, 1, 0, -1))
                    three2, three3 = read(triple, 1, 1), read(triple, 1, 0)
                    s1, s2, s3 = (read(smooth, 1, o) for o in (2, 1, 0))
                    z1, z2, z3 = (read(curve, 1, o) for o in (2, 1, 0))
                centre = source[i, at + back : at + back + 8, :]
                t0 = three2 - d1
                t1 = d2 + d3
                t2 = d4 - three3
                r0 = pl.reciprocal(s1 + t0 * t0, approx=True)
                r1 = pl.reciprocal(s2 + t1 * t1, approx=True)
                r2 = pl.reciprocal(s3 + t2 * t2, approx=True)
                w0 = r0 * (r0 * (1.0 / 3.0))
                w1 = r1 * r1
                w2 = r2 * r2
                above = (w0 + w0) * (z2 - z1) + w2 * (z3 - z2)
                below = (w0 + w2) + (w1 + w1)
                bent = above * pl.reciprocal(below, approx=True)
                line = t1 + d3
                if side == 0:
                    value = 6.0 * centre + line - bent
                else:
                    value = value + (6.0 * centre - line - bent)
            faces[i, begin : begin + 8, :] = value
        return carry

    lax.fori_loop(0, VARIABLES, upwind, 0)

    keep = lane_slots < live

    def back(index, carry):
        base = pl.multiple_of(index * 2 * GROUP, 2 * GROUP)
        high, low = [], []
        for v in range(VARIABLES):
            pieces = []
            for begin in (0, GROUP):
                here = faces[v, pl.ds(base + begin, GROUP), :]
                after = faces[v, pl.ds(base + begin + 1, GROUP), :]
                pieces.append(after - here)
            one, two = split(jnp.concatenate(pieces, axis=1))
            high.append(one)
            low.append(two)
        high = jnp.concatenate(high, axis=0)
        low = jnp.concatenate(low, axis=0)
        both = dot(right_high, high) + dot(right_high, low) + dot(right_low, high)
        both = both.reshape(VARIABLES, GROUP, 2 * slots)
        for part, begin in enumerate((0, GROUP)):
            piece = jnp.where(keep[None], both[:, :, part * slots : part * slots + slots], 0.0)
            one, two = split(piece)
            change[:, pl.ds(base + begin, GROUP), :slots] = one
            change[:, pl.ds(base + begin, GROUP), slots:] = two
        return carry

    lax.fori_loop(0, cells_z // (2 * GROUP), back, 0)

    for copy in incoming:
        copy.wait()

    def state(index, carry):
        at = pl.ds(pl.multiple_of(index * 8, 8), 8)
        pencil = index * 8 + lax.broadcasted_iota(jnp.int32, (8, slots), 0)
        calm = 1.0 - jnp.sum((wanted == pencil).astype(F32), axis=1, keepdims=True)
        for begin in range(0, cells_z, LANES):
            wide = slice(begin, begin + LANES)
            parts = [cells[v, at, wide] for v in range(VARIABLES)]
            inverse, pressure = state_of(parts)
            speed_y[at, wide] = parts[SPECIES + 1] * inverse
            press_y[at, wide] = pressure
            speed_z[at, wide] = parts[SPECIES + 2] * inverse * calm
            press_z[at, wide] = pressure * calm
        return carry

    lax.fori_loop(0, total // 8, state, 0)

    blocks = total // block_rows

    def advance(block, carry):
        base = pl.multiple_of(block * block_rows, block_rows)
        for v in range(VARIABLES):
            turn = v % 2
            for begin in range(0, block_rows, 16):
                at = pl.ds(base + begin, 16)
                value = cells[v, at, :]
                along_y = value * speed_y[at, :]
                along_z = value * speed_z[at, :]
                if v == SPECIES + 1:
                    along_y = along_y + press_y[at, :]
                if v == SPECIES + 2:
                    along_z = along_z + press_z[at, :]
                if v == SPECIES + 3:
                    along_y = along_y + press_y[at, :] * speed_y[at, :]
                    along_z = along_z + press_y[at, :] * speed_z[at, :]
                high, low = split(along_y)
                flux_y[turn, begin : begin + 16, :] = high
                flux_y[turn, block_rows + begin : block_rows + begin + 16, :] = low
                high, low = split(along_z)
                flux_z[turn, begin : begin + 16, :cells_z] = high
                flux_z[turn, begin : begin + 16, cells_z:] = low
            lanes = lax.broadcasted_iota(jnp.int32, (LANES, cells_z), 0) >> 3
            own = jnp.where(lanes == v, band_h[...], 0.0).astype(BF16)
            at = pl.ds(base, block_rows)
            gained = dot(flux_z[turn], band_z[...])
            gained = gained + dot(band_y[...], flux_y[turn])
            gained = gained + lax.dot_general(
                slot_hot[at, :], change[v], (((1,), (1,)), ((), ())), preferred_element_type=F32
            )
            gained = gained + dot(edge[at, :], jnp.concatenate([own, own], axis=0))
            cells[v, at, :] = cells[v, at, :] - (time_step / 60.0) * gained
        for x in range(block_rows // cells_y):
            pltpu.make_async_copy(
                cells.at[:, pl.ds(base + x * cells_y, cells_y), :],
                out_ref.at[:, block * (block_rows // cells_y) + x],
                out_sem,
            ).start()
        return carry

    lax.fori_loop(0, blocks, advance, 0)
    pltpu.make_async_copy(cells, cells, out_sem).wait()


def main(listed, count, conserved, face, char_left, char_right):
    _, cells_x, cells_y, cells_z = conserved.shape
    slots = listed.shape[0]
    total = cells_x * cells_y
    span = -(-(cells_z + 2 * LEAD) // GROUP) * GROUP
    block_rows = cells_y * max(1, min(cells_x, 256 // cells_y))
    vmem = pltpu.VMEM
    scratch = [
        vmem((VARIABLES, total, cells_z), F32),
        vmem((VARIABLES, slots, cells_z), F32),
        vmem((VARIABLES, span, slots), F32),
        vmem((span, slots), F32),
        vmem((span, slots), F32),
        vmem((VARIABLES, span + 8, slots), F32),
        vmem((VARIABLES, span + 8, slots), F32),
        vmem((2, span + 8, slots), F32),
        vmem((2, span + 8, slots), F32),
        vmem((2, span + 8, slots), F32),
        vmem((2, span + 8, slots), F32),
        vmem((VARIABLES, cells_z + 8, slots), F32),
        vmem((VARIABLES, cells_z, 2 * slots), BF16),
        vmem((total, 2 * LANES), BF16),
        vmem((LANES, total), F32),
        vmem((total, 2 * slots), BF16),
        vmem((total, cells_z), F32),
        vmem((total, cells_z), F32),
        vmem((total, cells_z), F32),
        vmem((total, cells_z), F32),
        vmem((2, block_rows, 2 * cells_z), BF16),
        vmem((2, 2 * block_rows, cells_z), BF16),
        vmem((block_rows, 2 * block_rows), BF16),
        vmem((2 * cells_z, cells_z), BF16),
        vmem((LANES, cells_z), F32),
        pltpu.SemaphoreType.DMA(()),
        pltpu.SemaphoreType.DMA((cells_x,)),
        pltpu.SemaphoreType.DMA(()),
    ]
    smem = pl.BlockSpec(memory_space=pltpu.SMEM)
    whole = pl.BlockSpec(memory_space=pltpu.VMEM)
    anywhere = pl.BlockSpec(memory_space=pl.ANY)
    return pl.pallas_call(
        main_kernel,
        out_shape=jax.ShapeDtypeStruct(conserved.shape, F32),
        in_specs=[smem, smem, anywhere, whole, whole, whole, whole],
        out_specs=anywhere,
        scratch_shapes=scratch,
        compiler_params=pltpu.CompilerParams(vmem_limit_bytes=56 << 20),
        cost_estimate=pl.CostEstimate(flops=8_000_000_000, bytes_accessed=16_000_000, transcendentals=4_000_000),
        name="section",
    )(listed, count, conserved, face, char_left, char_right, listed.reshape(1, slots))


def edge_kernel(out_in, before_ref, after_ref, out_ref, low_rows, high_rows, in_sem, out_sem):
    cells_x, cells_y = out_in.shape[1], out_in.shape[2]
    for x in range(cells_x):
        for j in range(WIDTH):
            pltpu.make_async_copy(
                out_in.at[:, x, pl.ds(j, 1), :], low_rows.at[j, :, pl.ds(x, 1), :], in_sem
            ).start()
            pltpu.make_async_copy(
                out_in.at[:, x, pl.ds(cells_y - WIDTH + j, 1), :], high_rows.at[j, :, pl.ds(x, 1), :], in_sem
            ).start()
    pltpu.make_async_copy(low_rows, low_rows, in_sem).wait()
    pltpu.make_async_copy(high_rows, high_rows, in_sem).wait()
    scale = time_step / 60.0
    for begin in range(0, out_in.shape[3], LANES):
        wide = slice(begin, begin + LANES)
        f0, f1, f2 = (flux_of([before_ref[j, v, :, wide] for v in range(VARIABLES)], 1) for j in range(WIDTH))
        for v in range(VARIABLES):
            low_rows[0, v, :, wide] += scale * (45.0 * f2[v] - 9.0 * f1[v] + f0[v])
            low_rows[1, v, :, wide] += scale * (f1[v] - 9.0 * f2[v])
            low_rows[2, v, :, wide] += scale * f2[v]
        f0, f1, f2 = (flux_of([after_ref[j, v, :, wide] for v in range(VARIABLES)], 1) for j in range(WIDTH))
        for v in range(VARIABLES):
            high_rows[2, v, :, wide] -= scale * (45.0 * f0[v] - 9.0 * f1[v] + f2[v])
            high_rows[1, v, :, wide] -= scale * (f1[v] - 9.0 * f0[v])
            high_rows[0, v, :, wide] -= scale * f0[v]
    for x in range(cells_x):
        for j in range(WIDTH):
            pltpu.make_async_copy(
                low_rows.at[j, :, pl.ds(x, 1), :], out_ref.at[:, x, pl.ds(j, 1), :], out_sem
            ).start()
            pltpu.make_async_copy(
                high_rows.at[j, :, pl.ds(x, 1), :], out_ref.at[:, x, pl.ds(cells_y - WIDTH + j, 1), :], out_sem
            ).start()
    pltpu.make_async_copy(low_rows, low_rows, out_sem).wait()
    pltpu.make_async_copy(high_rows, high_rows, out_sem).wait()


def add_edges(advanced, before, after):
    anywhere = pl.BlockSpec(memory_space=pl.ANY)
    whole = pl.BlockSpec(memory_space=pltpu.VMEM)
    return pl.pallas_call(
        edge_kernel,
        out_shape=jax.ShapeDtypeStruct(advanced.shape, F32),
        in_specs=[anywhere, whole, whole],
        out_specs=anywhere,
        scratch_shapes=[
            pltpu.VMEM(before.shape, F32),
            pltpu.VMEM(before.shape, F32),
            pltpu.SemaphoreType.DMA(()),
            pltpu.SemaphoreType.DMA(()),
        ],
        input_output_aliases={0: 0},
        cost_estimate=pl.CostEstimate(flops=5_000_000, bytes_accessed=2_000_000, transcendentals=0),
        name="edges",
    )(advanced, before, after)


def on_device(conserved, char_left, char_right, shock_list, shock_count):
    slots = shock_list.shape[-1]
    count = lax.axis_size("gy")
    ahead = [(i, (i + 1) % count) for i in range(count)]
    tail, head = pack_y(conserved)
    before = lax.ppermute(tail, "gy", ahead)
    after = lax.ppermute(head, "gy", [(b, a) for a, b in ahead])
    face = exchange_z(pack_z(conserved))
    advanced = main(
        shock_list.reshape(slots), shock_count.reshape(1), conserved, face, char_left, char_right
    )
    return add_edges(advanced, before, after)


def solution(mesh):
    placed = (P(None, "gx", "gy", "gz"), P(), P(), P("gx", "gy", "gz", None), P("gx", "gy", "gz"))
    return jax.shard_map(
        on_device, mesh=mesh, in_specs=placed, out_specs=P(None, "gx", "gy", "gz"), check_vma=False
    )
```

profile of v0, /device:TPU:0, one launch (start us, length us, event | category | flops | bytes accessed | tf_op | source)
XLA Modules:
  0.0 59.2 jit_solution(17127012733747945246)
XLA Ops:
  0.0 0.0 copy-start
  0.0 3.1 %copy-done = f32[14,8,64,256]{3,2,1,0:T(8,128)S(1)} copy-done((f32[14,8,64,256]{3,2,1,0:T(8,128)S(1)}, f32[14,8,64,256]{3,2,1,0:T(8,128)}, u32[]{:S(2)}) %copy-start) | copy-done | bytes 7340056
  3.1 2.1 %pack_z.1 = f32[512,128]{1,0:T(8,128)S(1)} custom-call(f32[14,8,64,256]{3,2,1,0:T(8,128)S(1)} %copy-done), custom_call_target="tpu_custom_call" | custom-call | flops 4000000 | bytes 7600000 | tf_op jit(solution)/shard_map/pack_z/pallas_call | solution.py:95
  5.2 0.5 collective-permute-start
  5.7 2.0 %pack_y.1 = (f32[3,14,8,256]{3,2,1,0:T(8,128)}, f32[3,14,8,256]{3,2,1,0:T(8,128)}) custom-call(f32[14,8,64,256]{3,2,1,0:T(8,128)} %u_ref.5), custom_call_target="tpu_custom_call" | custom-call | bytes 2000000 | tf_op jit(solution)/shard_map/pack_y/pallas_call | solution.py:72
  7.6 2.7 %collective-permute-start.1 = (f32[3,14,8,256]{3,2,1,0:T(8,128)}, f32[3,14,8,256]{3,2,1,0:T(8,128)S(1)}, u32[]{:S(2)}, u32[]{:S(2)}) collective-permute-start(f32[3,14,8,256]{3,2,1,0:T(8,128)} %get-tuple-element.7), channel_id=1, source_target_pairs={{0,2},{2,4},{4,6},{6,0},{1,3},{3,5},{5,7},{7,1},{8,10},{10,12},{12... | collective-permute-start | bytes 1032200 | tf_op jit(solution)/shard_map/ppermute | solution.py:552
  10.3 2.1 %collective-permute-start.2 = (f32[3,14,8,256]{3,2,1,0:T(8,128)}, f32[3,14,8,256]{3,2,1,0:T(8,128)S(1)}, u32[]{:S(2)}, u32[]{:S(2)}) collective-permute-start(f32[3,14,8,256]{3,2,1,0:T(8,128)} %get-tuple-element.8), channel_id=1, source_target_pairs={{2,0},{4,2},{6,4},{0,6},{3,1},{5,3},{7,5},{1,7},{10,8},{12,10},{14... | collective-permute-start | bytes 1032200 | tf_op jit(solution)/shard_map/ppermute | solution.py:553
  13.0 0.0 collective-permute-done.face_ref
  13.1 0.0 copy-start.3
  13.1 0.7 %copy-done.3 = f32[512,128]{1,0:T(8,128)} copy-done((f32[512,128]{1,0:T(8,128)}, f32[512,128]{1,0:T(8,128)S(1)}, u32[]{:S(2)}) %copy-start.3) | copy-done | bytes 262168
  13.8 40.8 %section.1.out_in = f32[14,8,64,256]{3,2,1,0:T(8,128)} custom-call(s32[128]{0:T(128)} %bitcast.4, s32[1]{0:T(128)} %bitcast.3.count_ref, f32[14,8,64,256]{3,2,1,0:T(8,128)} %u_ref.5, f32[512,128]{1,0:T(8,128)} %copy-done.3, f32[14,14]{1,0:T(8,128)} %left_ref.1, f32[14,14]{1,0:T(8,128)} %right_ref.1, s32[1,128]{1,0:T(1,128)} %bitcast.5), custom_call_target="tpu_custom_call" | custom-call | flops 8000000000 | bytes 16000000 | tf_op jit(solution)/shard_map/section/pallas_call | solution.py:478
  54.6 0.0 collective-permute-done.1.before_ref
  54.6 0.0 copy-start.1
  54.6 0.0 collective-permute-done.2.after_ref
  54.6 0.7 %copy-done.1 = f32[3,14,8,256]{3,2,1,0:T(8,128)} copy-done((f32[3,14,8,256]{3,2,1,0:T(8,128)}, f32[3,14,8,256]{3,2,1,0:T(8,128)S(1)}, u32[]{:S(2)}) %copy-start.1) | copy-done | bytes 344088
  55.4 0.0 copy-start.2
  55.4 0.7 %copy-done.2 = f32[3,14,8,256]{3,2,1,0:T(8,128)} copy-done((f32[3,14,8,256]{3,2,1,0:T(8,128)}, f32[3,14,8,256]{3,2,1,0:T(8,128)S(1)}, u32[]{:S(2)}) %copy-start.2) | copy-done | bytes 344088
  56.1 3.1 %edges.1 = f32[14,8,64,256]{3,2,1,0:T(8,128)} custom-call(f32[14,8,64,256]{3,2,1,0:T(8,128)} %section.1.out_in, f32[3,14,8,256]{3,2,1,0:T(8,128)} %copy-done.1, f32[3,14,8,256]{3,2,1,0:T(8,128)} %copy-done.2), custom_call_target="tpu_custom_call", output_to_operand_aliasing={{}: (0, {})} | custom-call | flops 5000000 | bytes 2000000 | tf_op jit(solution)/shard_map/edges/pallas_call | solution.py:530
Async XLA Ops:
  0.0 3.1 %copy-start = (f32[14,8,64,256]{3,2,1,0:T(8,128)S(1)}, f32[14,8,64,256]{3,2,1,0:T(8,128)}, u32[]{:S(2)}) copy-start(f32[14,8,64,256]{3,2,1,0:T(8,128)} %u_ref.5) | copy-start | bytes 22020100
  5.2 7.9 %collective-permute-start = (f32[512,128]{1,0:T(8,128)S(1)}, f32[512,128]{1,0:T(8,128)S(1)}, u32[]{:S(2)}, u32[]{:S(2)}) collective-permute-start(f32[512,128]{1,0:T(8,128)S(1)} %pack_z.1), channel_id=1, source_target_pairs={{0,1},{1,0},{2,3},{3,2},{4,5},{5,4},{6,7},{7,6},{8,9},{9,8},{10,11... | collective-permute-start | bytes 786440 | tf_op jit(solution)/shard_map/ppermute | solution.py:112
  7.6 47.0 %collective-permute-start.1 = (f32[3,14,8,256]{3,2,1,0:T(8,128)}, f32[3,14,8,256]{3,2,1,0:T(8,128)S(1)}, u32[]{:S(2)}, u32[]{:S(2)}) collective-permute-start(f32[3,14,8,256]{3,2,1,0:T(8,128)} %get-tuple-element.7), channel_id=1, source_target_pairs={{0,2},{2,4},{4,6},{6,0},{1,3},{3,5},{5,7},{7,1},{8,10},{10,12},{12... | collective-permute-start | bytes 1032200 | tf_op jit(solution)/shard_map/ppermute | solution.py:552
  10.3 44.3 %collective-permute-start.2 = (f32[3,14,8,256]{3,2,1,0:T(8,128)}, f32[3,14,8,256]{3,2,1,0:T(8,128)S(1)}, u32[]{:S(2)}, u32[]{:S(2)}) collective-permute-start(f32[3,14,8,256]{3,2,1,0:T(8,128)} %get-tuple-element.8), channel_id=1, source_target_pairs={{2,0},{4,2},{6,4},{0,6},{3,1},{5,3},{7,5},{1,7},{10,8},{12,10},{14... | collective-permute-start | bytes 1032200 | tf_op jit(solution)/shard_map/ppermute | solution.py:553
  13.1 0.7 %copy-start.3 = (f32[512,128]{1,0:T(8,128)}, f32[512,128]{1,0:T(8,128)S(1)}, u32[]{:S(2)}) copy-start(f32[512,128]{1,0:T(8,128)S(1)} %collective-permute-done.face_ref) | copy-start | bytes 786436
  54.6 0.7 %copy-start.1 = (f32[3,14,8,256]{3,2,1,0:T(8,128)}, f32[3,14,8,256]{3,2,1,0:T(8,128)S(1)}, u32[]{:S(2)}) copy-start(f32[3,14,8,256]{3,2,1,0:T(8,128)S(1)} %collective-permute-done.1.before_ref) | copy-start | bytes 1032196
  55.4 0.7 %copy-start.2 = (f32[3,14,8,256]{3,2,1,0:T(8,128)}, f32[3,14,8,256]{3,2,1,0:T(8,128)S(1)}, u32[]{:S(2)}) copy-start(f32[3,14,8,256]{3,2,1,0:T(8,128)S(1)} %collective-permute-done.2.after_ref) | copy-start | bytes 1032196
where the time goes:
time: 59.6 us; the launch traced here: 59.2 us
  Pallas kernels  48 us (81%)
  starting transfers between devices  5.27 us (9%)
  local copies, waits for them, and re-layouts  5.22 us (9%)
  between operations  0.72 us (1%)
    pallas_call x1, Pallas kernels, main(): pl.pallas_call(main_kernel, out_shape=jax.ShapeDtypeStruct(conserved.shap...  40.8 us
    unnamed x8, local copies, waits for them, and re-layouts  5.22 us
    pallas_call x1, Pallas kernels, add_edges(): pl.pallas_call(edge_kernel, out_shape=jax.ShapeDtypeStruct(advanced.shape...  3.15 us
    ppermute x1, starting transfers between devices, on_device(): before = lax.ppermute(tail, 'gy', ahead)  2.67 us
    ppermute x1, starting transfers between devices, on_device(): after = lax.ppermute(head, 'gy', [(b, a) for a, b in ahead])  2.09 us
    pallas_call x1, Pallas kernels, pack_z(): pl.pallas_call(pack_z_kernel, out_shape=jax.ShapeDtypeStruct((cells_x * c...  2.07 us
    pallas_call x1, Pallas kernels, pack_y(): pl.pallas_call(pack_y_kernel, out_shape=[face, face], in_specs=[pl.BlockS...  1.95 us
  transfers between devices with their start and end apart: 3, of which 0 were waited for; matrix products, arithmetic and copies ran while one was open for 0% of the time, Pallas kernels for 72%

commit v1 on v0

v1 whole, which is shorter than its diff:
```python
import functools

import jax
import jax.numpy as jnp
from jax import lax
from jax.experimental import pallas as pl
from jax.experimental.pallas import tpu as pltpu
from jax.sharding import PartitionSpec as P

SPECIES = 9
VARIABLES = 14
WIDTH = 3
GROUP = 16
LANES = 128
LEAD = 8

gas_excess = 0.4
time_step = 0.2
weno_epsilon = 1e-06

F32 = jnp.float32
BF16 = jnp.bfloat16


def split(values):
    high = values.astype(BF16)
    low = (values - high.astype(F32)).astype(BF16)
    return high, low


def dot(left, right):
    return jnp.dot(left, right, preferred_element_type=F32)


def state_of(parts):
    density = parts[0]
    for index in range(1, SPECIES):
        density = density + parts[index]
    inverse = pl.reciprocal(density, approx=True)
    first, second, last = parts[SPECIES], parts[SPECIES + 1], parts[SPECIES + 2]
    kinetic = 0.5 * (first * first + second * second + last * last) * inverse
    pressure = gas_excess * (parts[SPECIES + 3] - parts[SPECIES + 4] - kinetic)
    return inverse, pressure


def flux_of(parts, normal):
    inverse, pressure = state_of(parts)
    velocity = parts[SPECIES + normal] * inverse
    result = [part * velocity for part in parts]
    result[SPECIES + normal] = result[SPECIES + normal] + pressure
    result[SPECIES + 3] = result[SPECIES + 3] + pressure * velocity
    return result


def pack_y_kernel(u_ref, tail_ref, head_ref, sem):
    cells_x, cells_y = u_ref.shape[1], u_ref.shape[2]
    for x in range(cells_x):
        for j in range(WIDTH):
            pltpu.make_async_copy(
                u_ref.at[:, x, pl.ds(cells_y - WIDTH + j, 1), :], tail_ref.at[j, :, pl.ds(x, 1), :], sem
            ).start()
            pltpu.make_async_copy(
                u_ref.at[:, x, pl.ds(j, 1), :], head_ref.at[j, :, pl.ds(x, 1), :], sem
            ).start()
    pltpu.make_async_copy(tail_ref, tail_ref, sem).wait()
    pltpu.make_async_copy(head_ref, head_ref, sem).wait()


def pack_y(conserved):
    cells_x, cells_z = conserved.shape[1], conserved.shape[3]
    face = jax.ShapeDtypeStruct((WIDTH, VARIABLES, cells_x, cells_z), F32)
    return pl.pallas_call(
        pack_y_kernel,
        out_shape=[face, face],
        in_specs=[pl.BlockSpec(memory_space=pl.ANY)],
        out_specs=[pl.BlockSpec(memory_space=pltpu.VMEM)] * 2,
        scratch_shapes=[pltpu.SemaphoreType.DMA(())],
        cost_estimate=pl.CostEstimate(flops=0, bytes_accessed=2_000_000, transcendentals=0),
        name="pack_y",
    )(conserved)


def pack_z_kernel(u_ref, out_ref):
    cells_z = u_ref.shape[3]
    lane = lax.broadcasted_iota(jnp.int32, (u_ref.shape[2], LANES), 1)
    packed = jnp.zeros((u_ref.shape[2], LANES), F32)
    for v in range(VARIABLES):
        both = jnp.where(lane < LANES // 2, u_ref[v, 0, :, :LANES], u_ref[v, 0, :, cells_z - LANES :])
        packed = jnp.where(lane >> 3 == v, pltpu.roll(both, 8 * v + WIDTH, 1), packed)
    out_ref[...] = packed


def pack_z(conserved):
    _, cells_x, cells_y, cells_z = conserved.shape
    return pl.pallas_call(
        pack_z_kernel,
        out_shape=jax.ShapeDtypeStruct((cells_x * cells_y, LANES), F32),
        grid=(cells_x,),
        in_specs=[pl.BlockSpec((VARIABLES, 1, cells_y, cells_z), lambda x: (0, x, 0, 0))],
        out_specs=pl.BlockSpec((cells_y, LANES), lambda x: (x, 0)),
        compiler_params=pltpu.CompilerParams(vmem_limit_bytes=60 << 20),
        cost_estimate=pl.CostEstimate(flops=4_000_000, bytes_accessed=7_600_000, transcendentals=0),
        name="pack_z",
    )(conserved)


def exchange_z(packed):
    count = lax.axis_size("gz")
    if count == 1:
        return packed
    ahead = [(i, (i + 1) % count) for i in range(count)]
    from_left = lax.ppermute(packed, "gz", ahead)
    if count == 2:
        return from_left
    from_right = lax.ppermute(packed, "gz", [(b, a) for a, b in ahead])
    lane = jnp.arange(LANES, dtype=jnp.int32)[None, :]
    return jnp.where(lane & 7 < WIDTH, from_left, from_right)


def spread_matrix(matrix):
    rows = VARIABLES * GROUP
    pick = lax.broadcasted_iota(jnp.int32, (rows, VARIABLES), 0) >> 4
    pick = (pick == lax.broadcasted_iota(jnp.int32, (rows, VARIABLES), 1)).astype(F32)
    tall = jnp.dot(pick, matrix, precision=lax.Precision.HIGHEST, preferred_element_type=F32)
    wide = lax.dot_general(
        tall, pick, (((1,), (1,)), ((), ())), precision=lax.Precision.HIGHEST, preferred_element_type=F32
    )
    row = lax.broadcasted_iota(jnp.int32, (rows, rows), 0) & (GROUP - 1)
    column = lax.broadcasted_iota(jnp.int32, (rows, rows), 1) & (GROUP - 1)
    return split(jnp.where(row == column, wide, 0.0))


def stencil(offset):
    size = jnp.abs(offset)
    weight = jnp.where(size == 1, 45.0, jnp.where(size == 2, -9.0, jnp.where(size == 3, 1.0, 0.0)))
    return jnp.where(offset < 0, -weight, weight)


def shock_kernel(
    list_ref,
    count_ref,
    u_ref,
    face_ref,
    left_ref,
    right_ref,
    row_ref,
    change_ref,
    hot_ref,
    edge_ref,
    state_ref,
    cells,
    pencils,
    turned,
    speed_t,
    press_t,
    g_out,
    g_in,
    delta,
    triple,
    smooth,
    curve,
    third,
    faces,
    edge_t,
    near,
    picked_sem,
    in_sem,
    near_sem,
):
    _, cells_x, cells_y, cells_z = u_ref.shape
    slots = row_ref.shape[1]
    total = cells_x * cells_y
    span = turned.shape[1]
    nearby = pltpu.make_async_copy(face_ref, near, near_sem)
    nearby.start()

    def fetch(p, carry):
        place = list_ref[p]
        pltpu.make_async_copy(
            u_ref.at[:, place // cells_y, pl.ds(place % cells_y, 1), :], pencils.at[:, pl.ds(p, 1), :], picked_sem
        ).start()
        return carry

    lax.fori_loop(0, slots, fetch, 0)
    incoming = [
        pltpu.make_async_copy(u_ref.at[:, x], cells.at[:, pl.ds(x * cells_y, cells_y), :], in_sem.at[x])
        for x in range(cells_x)
    ]
    for copy in incoming:
        copy.start()

    left_high, left_low = spread_matrix(0.5 * left_ref[...])
    right_high, right_low = spread_matrix((time_step / 3.0) * right_ref[...])
    live = count_ref[0]
    lane_slots = lax.broadcasted_iota(jnp.int32, (1, slots), 1)
    wanted = jnp.where(lane_slots < live, row_ref[...], -1)
    scale = time_step / 60.0

    nearby.wait()
    for begin in range(0, total, LANES):
        edge_t[:, begin : begin + LANES] = near[begin : begin + LANES, :].T
    fluxes = flux_of([edge_t[8 * v : 8 * v + 8, :] for v in range(VARIABLES)], 2)
    for v in range(VARIABLES):
        edge_t[8 * v : 8 * v + 8, :] = fluxes[v]
    row = lax.broadcasted_iota(jnp.int32, (LANES, LANES), 0)
    column = lax.broadcasted_iota(jnp.int32, (LANES, LANES), 1)
    target, source = row & 7, column & 7
    reach = jnp.logical_xor(target < WIDTH, source < WIDTH)
    reach = reach & (target < 2 * WIDTH) & (source < 2 * WIDTH) & (row >> 3 == column >> 3)
    weights = jnp.where(reach, stencil(source - target), 0.0).astype(BF16)
    for begin in range(0, total, LANES):
        wide = slice(begin, begin + LANES)
        high, low = split(edge_t[:, wide])
        pencil = begin + lax.broadcasted_iota(jnp.int32, (LANES, slots), 0)
        hot = (wanted == pencil).astype(F32)
        calm = scale - scale * jnp.sum(hot, axis=1, keepdims=True)
        edge_ref[wide, :] = (dot(weights, high) + dot(weights, low)).T * calm
        hot = hot.astype(BF16)
        hot_ref[wide, :slots] = hot
        hot_ref[wide, slots:] = hot

    def neighbour(p, carry):
        speed_t[pl.ds(p, 1), :] = near[pl.ds(list_ref[p], 1), :]
        return carry

    lax.fori_loop(0, slots, neighbour, 0, unroll=8)
    border = speed_t[0:slots, :].T

    def state(index, carry):
        at = pl.ds(pl.multiple_of(index * 8, 8), 8)
        pencil = index * 8 + lax.broadcasted_iota(jnp.int32, (8, slots), 0)
        calm = scale - scale * jnp.sum((wanted == pencil).astype(F32), axis=1, keepdims=True)
        for begin in range(0, cells_z, LANES):
            wide = slice(begin, begin + LANES)
            parts = [cells[v, at, wide] for v in range(VARIABLES)]
            inverse, pressure = state_of(parts)
            state_ref[0, at, wide] = parts[SPECIES + 1] * (inverse * scale)
            state_ref[1, at, wide] = parts[SPECIES + 2] * (inverse * calm)
            state_ref[2, at, wide] = pressure
            state_ref[3, at, wide] = pressure * calm
        return carry

    for x in range(cells_x):
        incoming[x].wait()
        lax.fori_loop(x * cells_y // 8, (x + 1) * cells_y // 8, state, 0, unroll=True)

    pltpu.make_async_copy(pencils, pencils, picked_sem).wait()
    for v in range(VARIABLES):
        tile = border[8 * v : 8 * v + 8, :]
        turned[v, 0:LEAD, :] = tile
        turned[v, span - 8 : span, :] = tile
        turned[v, LEAD - WIDTH : LEAD - WIDTH + 8, :] = tile
        turned[v, LEAD + cells_z - WIDTH : LEAD + cells_z - WIDTH + 8, :] = tile
        for begin in range(0, cells_z, LANES):
            turned[v, LEAD + begin : LEAD + begin + LANES, :] = pencils[v, :, begin : begin + LANES].T

    top = jnp.zeros((8, slots), F32)
    for begin in range(0, span, 8):
        parts = [turned[v, begin : begin + 8, :] for v in range(VARIABLES)]
        inverse, pressure = state_of(parts)
        velocity = parts[SPECIES + 2] * inverse
        speed_t[begin : begin + 8, :] = 0.5 * velocity
        press_t[begin : begin + 8, :] = pressure
        size = jnp.abs(velocity)
        if begin < LEAD - WIDTH or begin + 8 > LEAD + cells_z + WIDTH:
            at = begin + lax.broadcasted_iota(jnp.int32, (8, slots), 0)
            size = jnp.where((at >= LEAD - WIDTH) & (at < LEAD + cells_z + WIDTH), size, 0.0)
        top = jnp.maximum(top, size)
    wave = 0.5 * (jnp.max(top, axis=0, keepdims=True) + 1.0)

    def project(index, carry):
        at = pl.ds(pl.multiple_of(index * GROUP, GROUP), GROUP)
        velocity = speed_t[at, :]
        pressure = press_t[at, :]
        parts = [turned[v, at, :] for v in range(VARIABLES)]
        flux = [part * velocity for part in parts]
        flux[SPECIES + 2] = flux[SPECIES + 2] + 0.5 * pressure
        flux[SPECIES + 3] = flux[SPECIES + 3] + pressure * velocity
        high, low = [], []
        for v in range(VARIABLES):
            one, two = split(jnp.concatenate([flux[v], wave * parts[v]], axis=1))
            high.append(one)
            low.append(two)
        high = jnp.concatenate(high, axis=0)
        low = jnp.concatenate(low, axis=0)
        both = dot(left_high, high) + dot(left_high, low) + dot(left_low, high)
        both = both.reshape(VARIABLES, GROUP, 2 * slots)
        g_out[:, at, :] = both[:, :, :slots] + both[:, :, slots:]
        g_in[:, at, :] = both[:, :, :slots] - both[:, :, slots:]
        return carry

    lax.fori_loop(0, span // GROUP, project, 0, unroll=True)

    def upwind(i, carry):
        for side, source in enumerate((g_out, g_in)):
            for begin in range(0, span, 8):
                step = source[i, begin + 1 : begin + 9, :] - source[i, begin : begin + 8, :]
                delta[side, begin : begin + 8, :] = step
                triple[side, begin : begin + 8, :] = 3.0 * step
            for begin in range(1, span, 8):
                bend = delta[side, begin : begin + 8, :] - delta[side, begin - 1 : begin + 7, :]
                curve[side, begin : begin + 8, :] = bend
                smooth[side, begin : begin + 8, :] = (13.0 / 3.0 * bend) * bend + weno_epsilon
            for begin in range(0, span, 8):
                third[side, begin : begin + 8, :] = (
                    curve[side, begin + 1 : begin + 9, :] - curve[side, begin : begin + 8, :]
                )
        for begin in range(0, cells_z + 8, 8):
            at = begin + LEAD - 1

            def read(ref, side, offset):
                return ref[side, at + offset : at + offset + 8, :]

            value = None
            for side, source in enumerate((g_out, g_in)):
                if side == 0:
                    d1, d2, d3, d4 = (read(delta, 0, o) for o in (-2, -1, 0, 1))
                    three2, three3 = read(triple, 0, -1), read(triple, 0, 0)
                    s1, s2, s3 = (read(smooth, 0, o) for o in (-1, 0, 1))
                    u1, u2 = (read(third, 0, o) for o in (-1, 0))
                else:
                    d1, d2, d3, d4 = (read(delta, 1, o) for o in (2, 1, 0, -1))
                    three2, three3 = read(triple, 1, 1), read(triple, 1, 0)
                    s1, s2, s3 = (read(smooth, 1, o) for o in (2, 1, 0))
                    u1, u2 = (read(third, 1, o) for o in (1, 0))
                centre = source[i, at + side : at + side + 8, :]
                t0 = three2 - d1
                t1 = d2 + d3
                t2 = d4 - three3
                r0 = pl.reciprocal(s1 + t0 * t0, approx=True)
                r1 = pl.reciprocal(s2 + t1 * t1, approx=True)
                r2 = pl.reciprocal(s3 + t2 * t2, approx=True)
                w0 = r0 * (r0 * (1.0 / 3.0))
                w1 = r1 * r1
                w2 = r2 * r2
                above = (w0 + w0) * u1 + w2 * u2
                below = (w0 + w2) + (w1 + w1)
                bent = above * pl.reciprocal(below, approx=True)
                line = t1 + d3
                if side == 0:
                    value = 6.0 * centre + line - bent
                else:
                    value = value + (6.0 * centre - line + bent)
            faces[i, begin : begin + 8, :] = value
        return carry

    lax.fori_loop(0, VARIABLES, upwind, 0)

    keep = lane_slots < live

    def back(index, carry):
        base = pl.multiple_of(index * 2 * GROUP, 2 * GROUP)
        high, low = [], []
        for v in range(VARIABLES):
            pieces = []
            for begin in (0, GROUP):
                here = faces[v, pl.ds(base + begin, GROUP), :]
                after = faces[v, pl.ds(base + begin + 1, GROUP), :]
                pieces.append(after - here)
            one, two = split(jnp.concatenate(pieces, axis=1))
            high.append(one)
            low.append(two)
        high = jnp.concatenate(high, axis=0)
        low = jnp.concatenate(low, axis=0)
        both = dot(right_high, high) + dot(right_high, low) + dot(right_low, high)
        both = both.reshape(VARIABLES, GROUP, 2 * slots)
        for part, begin in enumerate((0, GROUP)):
            piece = jnp.where(keep[None], both[:, :, part * slots : part * slots + slots], 0.0)
            one, two = split(piece)
            change_ref[:, pl.ds(base + begin, GROUP), :slots] = one
            change_ref[:, pl.ds(base + begin, GROUP), slots:] = two
        return carry

    lax.fori_loop(0, cells_z // (2 * GROUP), back, 0, unroll=True)


def shock(listed, count, conserved, face, char_left, char_right):
    _, cells_x, cells_y, cells_z = conserved.shape
    slots = listed.shape[0]
    total = cells_x * cells_y
    span = -(-(cells_z + 2 * LEAD) // GROUP) * GROUP
    vmem = pltpu.VMEM
    work = vmem((2, span + 8, slots), F32)
    scratch = [
        vmem((VARIABLES, total, cells_z), F32),
        vmem((VARIABLES, slots, cells_z), F32),
        vmem((VARIABLES, span, slots), F32),
        vmem((span, slots), F32),
        vmem((span, slots), F32),
        vmem((VARIABLES, span + 8, slots), F32),
        vmem((VARIABLES, span + 8, slots), F32),
        work,
        work,
        work,
        work,
        work,
        vmem((VARIABLES, cells_z + 8, slots), F32),
        vmem((LANES, total), F32),
        vmem((total, LANES), F32),
        pltpu.SemaphoreType.DMA(()),
        pltpu.SemaphoreType.DMA((cells_x,)),
        pltpu.SemaphoreType.DMA(()),
    ]
    smem = pl.BlockSpec(memory_space=pltpu.SMEM)
    whole = pl.BlockSpec(memory_space=pltpu.VMEM)
    anywhere = pl.BlockSpec(memory_space=pl.ANY)
    return pl.pallas_call(
        shock_kernel,
        out_shape=[
            jax.ShapeDtypeStruct((VARIABLES, cells_z, 2 * slots), BF16),
            jax.ShapeDtypeStruct((total, 2 * slots), BF16),
            jax.ShapeDtypeStruct((total, LANES), F32),
            jax.ShapeDtypeStruct((4, total, cells_z), F32),
        ],
        in_specs=[smem, smem, anywhere, anywhere, whole, whole, whole],
        out_specs=[whole] * 4,
        scratch_shapes=scratch,
        compiler_params=pltpu.CompilerParams(vmem_limit_bytes=48 << 20),
        cost_estimate=pl.CostEstimate(flops=6_000_000_000, bytes_accessed=14_000_000, transcendentals=4_000_000),
        name="shock",
    )(listed, count, conserved, face, char_left, char_right, listed.reshape(1, slots))


def advance_kernel(
    u_ref, change_ref, hot_ref, edge_ref, state_ref, before_ref, after_ref, out_ref, fluxes, along_y, around, band
):
    total, cells_z = u_ref.shape[1], u_ref.shape[2]
    cells_x = before_ref.shape[2]
    cells_y = total // cells_x
    pitch = cells_y + 16
    v = pl.program_id(0)
    scale = time_step / 60.0
    normal_y = v == SPECIES + 1
    normal_z = v == SPECIES + 2
    energy = v == SPECIES + 3

    @pl.when(v == 0)
    def _():
        row = lax.broadcasted_iota(jnp.int32, (cells_z, cells_z), 0)
        column = lax.broadcasted_iota(jnp.int32, (cells_z, cells_z), 1)
        weights = stencil(row - column).astype(BF16)
        band[:cells_z, :] = weights
        band[cells_z:, :] = weights
        for side, source in enumerate((before_ref, after_ref)):
            for j in range(WIDTH):
                for begin in range(0, cells_z, LANES):
                    wide = slice(begin, begin + LANES)
                    parts = [source[j, i, :, wide] for i in range(VARIABLES)]
                    inverse, pressure = state_of(parts)
                    around[side, j, 0, :, wide] = parts[SPECIES + 1] * (inverse * scale)
                    around[side, j, 1, :, wide] = pressure

    def fill(extra_y, extra_z):
        for side, source in enumerate((before_ref, after_ref)):
            for j in range(WIDTH):
                for half in range(cells_z // LANES):
                    wide = slice(half * LANES, half * LANES + LANES)
                    value = source[j, v, :, wide]
                    value = extra_y(value, around[side, j, 0, :, wide], around[side, j, 1, :, wide])
                    begin = 8 - WIDTH + j if side == 0 else 8 + cells_y + j
                    along_y[half, pl.ds(begin, cells_x, stride=pitch), :] = value
        for begin in range(0, total, GROUP):
            at = slice(begin, begin + GROUP)
            place = begin // cells_y * pitch + 8 + begin % cells_y
            for half in range(cells_z // LANES):
                wide = slice(half * LANES, half * LANES + LANES)
                value = u_ref[0, at, wide]
                along_y[half, place : place + GROUP, :] = extra_y(value, state_ref[0, at, wide], state_ref[2, at, wide])
                high, low = split(extra_z(value, state_ref[1, at, wide], at, wide))
                fluxes[at, half * LANES : half * LANES + LANES] = high
                fluxes[at, cells_z + half * LANES : cells_z + half * LANES + LANES] = low

    plain_y = lambda value, speed, pressure: value * speed
    plain_z = lambda value, speed, at, wide: value * speed

    @pl.when(jnp.logical_not(normal_y | normal_z | energy))
    def _():
        fill(plain_y, plain_z)

    @pl.when(normal_y)
    def _():
        fill(lambda value, speed, pressure: value * speed + scale * pressure, plain_z)

    @pl.when(normal_z)
    def _():
        fill(plain_y, lambda value, speed, at, wide: value * speed + state_ref[3, at, wide])

    @pl.when(energy)
    def _():
        fill(
            lambda value, speed, pressure: (value + pressure) * speed,
            lambda value, speed, at, wide: (value + state_ref[2, at, wide]) * speed,
        )

    lane = lax.broadcasted_iota(jnp.int32, (GROUP, LANES), 1)
    turn = (LANES - WIDTH - 8 * v) & (LANES - 1)
    rows = min(total, 256)
    for base in range(0, total, rows):
        gained = dot(fluxes[base : base + rows, :], band[...])
        gained = gained + lax.dot_general(
            hot_ref[base : base + rows, :], change_ref[0], (((1,), (1,)), ((), ())), preferred_element_type=F32
        )
        for begin in range(base, base + rows, GROUP):
            at = slice(begin, begin + GROUP)
            place = begin // cells_y * pitch + 8 + begin % cells_y
            border = pltpu.roll(edge_ref[at, :], turn, 1)
            for half in range(cells_z // LANES):
                wide = slice(half * LANES, half * LANES + LANES)

                def read(offset):
                    return along_y[half, place + offset : place + offset + GROUP, :]

                value = u_ref[0, at, wide] - gained[begin - base : begin - base + GROUP, wide]
                value = value - (
                    45.0 * (read(1) - read(-1)) - 9.0 * (read(2) - read(-2)) + (read(3) - read(-3))
                )
                if half == 0:
                    value = value - jnp.where(lane < WIDTH, border, 0.0)
                if half == cells_z // LANES - 1:
                    value = value - jnp.where(lane >= LANES - WIDTH, border, 0.0)
                out_ref[0, at, wide] = value


def advance(conserved, change, hot, edge, state, before, after):
    _, cells_x, cells_y, cells_z = conserved.shape
    total = cells_x * cells_y
    one = pl.BlockSpec((1, total, cells_z), lambda v: (v, 0, 0))

    def fixed(array):
        return pl.BlockSpec(array.shape, lambda v: (0,) * array.ndim)

    result = pl.pallas_call(
        advance_kernel,
        out_shape=jax.ShapeDtypeStruct((VARIABLES, total, cells_z), F32),
        grid=(VARIABLES,),
        in_specs=[
            one,
            pl.BlockSpec((1,) + change.shape[1:], lambda v: (v, 0, 0)),
            fixed(hot),
            fixed(edge),
            fixed(state),
            fixed(before),
            fixed(after),
        ],
        out_specs=one,
        scratch_shapes=[
            pltpu.VMEM((total, 2 * cells_z), BF16),
            pltpu.VMEM((cells_z // LANES, cells_x * (cells_y + 16), LANES), F32),
            pltpu.VMEM((2, WIDTH, 2, cells_x, cells_z), F32),
            pltpu.VMEM((2 * cells_z, cells_z), BF16),
        ],
        compiler_params=pltpu.CompilerParams(vmem_limit_bytes=24 << 20),
        cost_estimate=pl.CostEstimate(flops=4_000_000_000, bytes_accessed=20_000_000, transcendentals=0),
        name="advance",
    )(conserved.reshape(VARIABLES, total, cells_z), change, hot, edge, state, before, after)
    return result.reshape(conserved.shape)


def on_device(conserved, char_left, char_right, shock_list, shock_count):
    slots = shock_list.shape[-1]
    count = lax.axis_size("gy")
    ahead = [(i, (i + 1) % count) for i in range(count)]
    tail, head = pack_y(conserved)
    before = lax.ppermute(tail, "gy", ahead)
    after = lax.ppermute(head, "gy", [(b, a) for a, b in ahead])
    face = exchange_z(pack_z(conserved))
    change, hot, edge, state = shock(
        shock_list.reshape(slots), shock_count.reshape(1), conserved, face, char_left, char_right
    )
    return advance(conserved, change, hot, edge, state, before, after)


def solution(mesh):
    placed = (P(None, "gx", "gy", "gz"), P(), P(), P("gx", "gy", "gz", None), P("gx", "gy", "gz"))
    return jax.shard_map(
        on_device, mesh=mesh, in_specs=placed, out_specs=P(None, "gx", "gy", "gz"), check_vma=False
    )
```

time: 59.6 us -> 41.6 us (0.70)
  Pallas kernels: 48 us -> 35.4 us
  local copies, waits for them, and re-layouts: 5.22 us -> 0.02 us
    pallas_call x2, Pallas kernels: 44 us -> 26.3 us  [the longest x1 15 us: shock(): pl.pallas_call(shock_kernel, out_shape=[jax.ShapeDtypeStruct((VARIABLES,...]
    unnamed x8 -> x10, local copies, waits for them, and re-layouts: 5.22 us -> 0.02 us
    pallas_call x1, Pallas kernels: 2.07 us -> 6.97 us  [pack_z(): pl.pallas_call(pack_z_kernel, out_shape=jax.ShapeDtypeStruct((cells_x * c...]
  transfers between devices with their start and end apart: 3 -> 3, of which waited for: 0 -> 0; matrix products, arithmetic and copies ran while one was open for 0% -> 0% of each run, Pallas kernels for 72% -> 41%
where the time goes in v1:
time: 41.6 us; the launch traced here: 41.3 us
  Pallas kernels  35.4 us (85%)
  starting transfers between devices  5.17 us (12%)
  between operations  0.75 us (2%)
    pallas_call x1, Pallas kernels, shock(): pl.pallas_call(shock_kernel, out_shape=[jax.ShapeDtypeStruct((VARIABLES,...  15 us
    pallas_call x1, Pallas kernels, advance(): pl.pallas_call(advance_kernel, out_shape=jax.ShapeDtypeStruct((VARIABLES,...  11.3 us
    pallas_call x1, Pallas kernels, pack_z(): pl.pallas_call(pack_z_kernel, out_shape=jax.ShapeDtypeStruct((cells_x * c...  6.97 us
    ppermute x1, starting transfers between devices, on_device(): before = lax.ppermute(tail, 'gy', ahead)  2.63 us
    ppermute x1, starting transfers between devices, on_device(): after = lax.ppermute(head, 'gy', [(b, a) for a, b in ahead])  2.09 us
    pallas_call x1, Pallas kernels, pack_y(): pl.pallas_call(pack_y_kernel, out_shape=[face, face], in_specs=[pl.BlockS...  2.07 us
  transfers between devices with their start and end apart: 3, of which 0 were waited for; matrix products, arithmetic and copies ran while one was open for 0% of the time, Pallas kernels for 41%

profile of v1, /device:TPU:0, one launch (start us, length us, event | category | flops | bytes accessed | tf_op | source)
XLA Modules:
  0.0 41.3 jit_solution(15920906780012356709)
XLA Ops:
  0.0 0.0 copy-start.2
  0.0 0.0 copy-start.1
  0.0 0.0 copy-start
  0.0 7.0 %pack_z.1 = f32[512,128]{1,0:T(8,128)} custom-call(f32[14,8,64,256]{3,2,1,0:T(8,128)} %u_ref.5), custom_call_target="tpu_custom_call" | custom-call | flops 4000000 | bytes 7600000 | tf_op jit(solution)/shard_map/pack_z/pallas_call | solution.py:95
  7.0 0.5 %collective-permute-start = (f32[512,128]{1,0:T(8,128)}, f32[512,128]{1,0:T(8,128)S(1)}, u32[]{:S(2)}, u32[]{:S(2)}) collective-permute-start(f32[512,128]{1,0:T(8,128)} %pack_z.1), channel_id=1, source_target_pairs={{0,1},{1,0},{2,3},{3,2},{4,5},{5,4},{6,7},{7,6},{8,9},{9,8},{10,11... | collective-permute-start | bytes 786440 | tf_op jit(solution)/shard_map/ppermute | solution.py:112
  7.4 0.0 slice-start
  7.4 2.1 %pack_y.1 = (f32[3,14,8,256]{3,2,1,0:T(8,128)}, f32[3,14,8,256]{3,2,1,0:T(8,128)}) custom-call(f32[14,8,64,256]{3,2,1,0:T(8,128)} %u_ref.5), custom_call_target="tpu_custom_call" | custom-call | bytes 2000000 | tf_op jit(solution)/shard_map/pack_y/pallas_call | solution.py:72
  9.5 2.6 %collective-permute-start.1 = (f32[3,14,8,256]{3,2,1,0:T(8,128)}, f32[3,14,8,256]{3,2,1,0:T(8,128)S(1)}, u32[]{:S(2)}, u32[]{:S(2)}) collective-permute-start(f32[3,14,8,256]{3,2,1,0:T(8,128)} %get-tuple-element.15), channel_id=1, source_target_pairs={{0,2},{2,4},{4,6},{6,0},{1,3},{3,5},{5,7},{7,1},{8,10},{10,12},{12... | collective-permute-start | bytes 1032200 | tf_op jit(solution)/shard_map/ppermute | solution.py:564
  12.1 2.1 %collective-permute-start.2 = (f32[3,14,8,256]{3,2,1,0:T(8,128)}, f32[3,14,8,256]{3,2,1,0:T(8,128)S(1)}, u32[]{:S(2)}, u32[]{:S(2)}) collective-permute-start(f32[3,14,8,256]{3,2,1,0:T(8,128)} %get-tuple-element.16), channel_id=1, source_target_pairs={{2,0},{4,2},{6,4},{0,6},{3,1},{5,3},{7,5},{1,7},{10,8},{12,10},{14... | collective-permute-start | bytes 1032200 | tf_op jit(solution)/shard_map/ppermute | solution.py:565
  14.9 0.0 collective-permute-done.face_ref
  14.9 0.0 copy-done.2
  14.9 0.0 copy-done.1
  14.9 0.0 copy-done
  14.9 0.0 slice-start.1
  14.9 15.0 %shock.1 = (bf16[14,256,256]{2,1,0:T(8,128)(2,1)S(1)}, bf16[512,256]{1,0:T(8,128)(2,1)S(1)}, f32[512,128]{1,0:T(8,128)S(1)}, f32[4,512,256]{2,1,0:T(8,128)S(1)}) custom-call(s32[128]{0:T(128)S(1)} %bitcast.9, s32[1]{0:T(128)} %bitcast.5.count_ref, f32[14,8,64,256]{3,2,1,0:T(8,128)} %u_ref.5, f32[512,128]{1,0:T(8,128)S(1)} %collective-permute-done.face_ref, ...), custom_call_target="tpu_custom_call" | custom-call | flops 6000000000 | bytes 14000000 | tf_op jit(solution)/shard_map/shock/pallas_call | solution.py:407
  29.9 0.0 collective-permute-done.1.before_ref
  30.0 0.0 collective-permute-done.2.after_ref
  30.0 0.0 slice-done
  30.0 0.0 slice-done.1
  30.0 11.3 %advance.1 = f32[14,512,256]{2,1,0:T(8,128)} custom-call(f32[14,512,256]{2,1,0:T(8,128)S(1)} %bitcast.8, bf16[14,256,256]{2,1,0:T(8,128)(2,1)S(1)} %get-tuple-element.11.change_ref, bf16[512,256]{1,0:T(8,128)(2,1)S(1)} %get-tuple-element.12.hot_ref, f32[512,128]{1,0:T(8,128)S(1)} %get-tuple-element.13.edge_ref, ...), custom_call_target="tpu_custom_call" | custom-call | flops 4000000000 | bytes 20000000 | tf_op jit(solution)/shard_map/advance/pallas_call | solution.py:532
  (1 shorter events, 0.0 us)
Async XLA Ops:
  0.0 14.9 %copy-start.2 = (s32[1,1,1,128]{3,2,1,0:T(1,128)S(1)}, s32[1,1,1,128]{3,2,1,0:T(1,128)}, u32[]{:S(2)}) copy-start(s32[1,1,1,128]{3,2,1,0:T(1,128)} %param.8) | copy-start | bytes 1540
  0.0 14.9 %copy-start.1 = (f32[14,14]{1,0:T(8,128)S(1)}, f32[14,14]{1,0:T(8,128)}, u32[]{:S(2)}) copy-start(f32[14,14]{1,0:T(8,128)} %right_ref.1) | copy-start | bytes 2356
  0.0 14.9 %copy-start = (f32[14,14]{1,0:T(8,128)S(1)}, f32[14,14]{1,0:T(8,128)}, u32[]{:S(2)}) copy-start(f32[14,14]{1,0:T(8,128)} %left_ref.1) | copy-start | bytes 2356
  7.0 7.9 %collective-permute-start = (f32[512,128]{1,0:T(8,128)}, f32[512,128]{1,0:T(8,128)S(1)}, u32[]{:S(2)}, u32[]{:S(2)}) collective-permute-start(f32[512,128]{1,0:T(8,128)} %pack_z.1), channel_id=1, source_target_pairs={{0,1},{1,0},{2,3},{3,2},{4,5},{5,4},{6,7},{7,6},{8,9},{9,8},{10,11... | collective-permute-start | bytes 786440 | tf_op jit(solution)/shard_map/ppermute | solution.py:112
  7.4 22.5 %slice-start = ((s8[7340032]{0:T(1024)(128)(4,1)}), s8[3145728]{0:T(1024)(128)(4,1)S(1)}, s32[]{:S(2)}) async-start(s8[7340032]{0:T(1024)(128)(4,1)} %bitcast.6), calls=%async_computation | async-start | bytes 6291456
  9.5 20.4 %collective-permute-start.1 = (f32[3,14,8,256]{3,2,1,0:T(8,128)}, f32[3,14,8,256]{3,2,1,0:T(8,128)S(1)}, u32[]{:S(2)}, u32[]{:S(2)}) collective-permute-start(f32[3,14,8,256]{3,2,1,0:T(8,128)} %get-tuple-element.15), channel_id=1, source_target_pairs={{0,2},{2,4},{4,6},{6,0},{1,3},{3,5},{5,7},{7,1},{8,10},{10,12},{12... | collective-permute-start | bytes 1032200 | tf_op jit(solution)/shard_map/ppermute | solution.py:564
  12.1 17.8 %collective-permute-start.2 = (f32[3,14,8,256]{3,2,1,0:T(8,128)}, f32[3,14,8,256]{3,2,1,0:T(8,128)S(1)}, u32[]{:S(2)}, u32[]{:S(2)}) collective-permute-start(f32[3,14,8,256]{3,2,1,0:T(8,128)} %get-tuple-element.16), channel_id=1, source_target_pairs={{2,0},{4,2},{6,4},{0,6},{3,1},{5,3},{7,5},{1,7},{10,8},{12,10},{14... | collective-permute-start | bytes 1032200 | tf_op jit(solution)/shard_map/ppermute | solution.py:565
  14.9 15.0 %slice-start.1 = ((s8[7340032]{0:T(1024)(128)(4,1)}), s8[4194304]{0:T(1024)(128)(4,1)S(1)}, s32[]{:S(2)}) async-start(s8[7340032]{0:T(1024)(128)(4,1)} %bitcast.6), calls=%async_computation.1 | async-start | bytes 8388608

commit v2 on v1

--- a/solution.py
+++ b/solution.py
@@ -52,55 +52,39 @@
     return result
 
 
-def pack_y_kernel(u_ref, tail_ref, head_ref, sem):
-    cells_x, cells_y = u_ref.shape[1], u_ref.shape[2]
+def pack_kernel(u_ref, tail_ref, head_ref, face_ref, row_sem):
+    _, cells_x, cells_y, cells_z = u_ref.shape
     for x in range(cells_x):
         for j in range(WIDTH):
             pltpu.make_async_copy(
-                u_ref.at[:, x, pl.ds(cells_y - WIDTH + j, 1), :], tail_ref.at[j, :, pl.ds(x, 1), :], sem
+                u_ref.at[:, x, pl.ds(cells_y - WIDTH + j, 1), :], tail_ref.at[j, :, pl.ds(x, 1), :], row_sem
             ).start()
             pltpu.make_async_copy(
-                u_ref.at[:, x, pl.ds(j, 1), :], head_ref.at[j, :, pl.ds(x, 1), :], sem
+                u_ref.at[:, x, pl.ds(j, 1), :], head_ref.at[j, :, pl.ds(x, 1), :], row_sem
             ).start()
-    pltpu.make_async_copy(tail_ref, tail_ref, sem).wait()
-    pltpu.make_async_copy(head_ref, head_ref, sem).wait()
-
-
-def pack_y(conserved):
-    cells_x, cells_z = conserved.shape[1], conserved.shape[3]
-    face = jax.ShapeDtypeStruct((WIDTH, VARIABLES, cells_x, cells_z), F32)
+    lane = lax.broadcasted_iota(jnp.int32, (cells_y, LANES), 1)
+    for x in range(cells_x):
+        packed = jnp.zeros((cells_y, LANES), F32)
+        for v in range(VARIABLES):
+            both = jnp.where(lane < LANES // 2, u_ref[v, x, :, :LANES], u_ref[v, x, :, cells_z - LANES :])
+            packed = jnp.where(lane >> 3 == v, pltpu.roll(both, 8 * v + WIDTH, 1), packed)
+        face_ref[x * cells_y : (x + 1) * cells_y, :] = packed
+    pltpu.make_async_copy(tail_ref, tail_ref, row_sem).wait()
+    pltpu.make_async_copy(head_ref, head_ref, row_sem).wait()
+
+
+def pack(conserved):
+    _, cells_x, cells_y, cells_z = conserved.shape
+    rows = jax.ShapeDtypeStruct((WIDTH, VARIABLES, cells_x, cells_z), F32)
     return pl.pallas_call(
-        pack_y_kernel,
-        out_shape=[face, face],
-        in_specs=[pl.BlockSpec(memory_space=pl.ANY)],
-        out_specs=[pl.BlockSpec(memory_space=pltpu.VMEM)] * 2,
+        pack_kernel,
+        out_shape=[rows, rows, jax.ShapeDtypeStruct((cells_x * cells_y, LANES), F32)],
+        in_specs=[pl.BlockSpec(memory_space=pltpu.VMEM)],
+        out_specs=[pl.BlockSpec(memory_space=pltpu.VMEM)] * 3,
         scratch_shapes=[pltpu.SemaphoreType.DMA(())],
-        cost_estimate=pl.CostEstimate(flops=0, bytes_accessed=2_000_000, transcendentals=0),
-        name="pack_y",
-    )(conserved)
-
-
-def pack_z_kernel(u_ref, out_ref):
-    cells_z = u_ref.shape[3]
-    lane = lax.broadcasted_iota(jnp.int32, (u_ref.shape[2], LANES), 1)
-    packed = jnp.zeros((u_ref.shape[2], LANES), F32)
-    for v in range(VARIABLES):
-        both = jnp.where(lane < LANES // 2, u_ref[v, 0, :, :LANES], u_ref[v, 0, :, cells_z - LANES :])
-        packed = jnp.where(lane >> 3 == v, pltpu.roll(both, 8 * v + WIDTH, 1), packed)
-    out_ref[...] = packed
-
-
-def pack_z(conserved):
-    _, cells_x, cells_y, cells_z = conserved.shape
-    return pl.pallas_call(
-        pack_z_kernel,
-        out_shape=jax.ShapeDtypeStruct((cells_x * cells_y, LANES), F32),
-        grid=(cells_x,),
-        in_specs=[pl.BlockSpec((VARIABLES, 1, cells_y, cells_z), lambda x: (0, x, 0, 0))],
-        out_specs=pl.BlockSpec((cells_y, LANES), lambda x: (x, 0)),
-        compiler_params=pltpu.CompilerParams(vmem_limit_bytes=60 << 20),
-        cost_estimate=pl.CostEstimate(flops=4_000_000, bytes_accessed=7_600_000, transcendentals=0),
-        name="pack_z",
+        compiler_params=pltpu.CompilerParams(vmem_limit_bytes=16 << 20),
+        cost_estimate=pl.CostEstimate(flops=4_000_000, bytes_accessed=9_000_000, transcendentals=0),
+        name="pack",
     )(conserved)
 
 
@@ -148,7 +132,6 @@
     hot_ref,
     edge_ref,
     state_ref,
-    cells,
     pencils,
     turned,
     speed_t,
@@ -162,17 +145,12 @@
     third,
     faces,
     edge_t,
-    near,
     picked_sem,
-    in_sem,
-    near_sem,
 ):
     _, cells_x, cells_y, cells_z = u_ref.shape
     slots = row_ref.shape[1]
     total = cells_x * cells_y
     span = turned.shape[1]
-    nearby = pltpu.make_async_copy(face_ref, near, near_sem)
-    nearby.start()
 
     def fetch(p, carry):
         place = list_ref[p]
@@ -182,13 +160,6 @@
         return carry
 
     lax.fori_loop(0, slots, fetch, 0)
-    incoming = [
-        pltpu.make_async_copy(u_ref.at[:, x], cells.at[:, pl.ds(x * cells_y, cells_y), :], in_sem.at[x])
-        for x in range(cells_x)
-    ]
-    for copy in incoming:
-        copy.start()
-
     left_high, left_low = spread_matrix(0.5 * left_ref[...])
     right_high, right_low = spread_matrix((time_step / 3.0) * right_ref[...])
     live = count_ref[0]
@@ -196,9 +167,8 @@
     wanted = jnp.where(lane_slots < live, row_ref[...], -1)
     scale = time_step / 60.0
 
-    nearby.wait()
     for begin in range(0, total, LANES):
-        edge_t[:, begin : begin + LANES] = near[begin : begin + LANES, :].T
+        edge_t[:, begin : begin + LANES] = face_ref[begin : begin + LANES, :].T
     fluxes = flux_of([edge_t[8 * v : 8 * v + 8, :] for v in range(VARIABLES)], 2)
     for v in range(VARIABLES):
         edge_t[8 * v : 8 * v + 8, :] = fluxes[v]
@@ -220,19 +190,20 @@
         hot_ref[wide, slots:] = hot
 
     def neighbour(p, carry):
-        speed_t[pl.ds(p, 1), :] = near[pl.ds(list_ref[p], 1), :]
+        speed_t[pl.ds(p, 1), :] = face_ref[pl.ds(list_ref[p], 1), :]
         return carry
 
     lax.fori_loop(0, slots, neighbour, 0, unroll=8)
     border = speed_t[0:slots, :].T
 
     def state(index, carry):
-        at = pl.ds(pl.multiple_of(index * 8, 8), 8)
+        at = slice(index * 8, index * 8 + 8)
+        x, y = index * 8 // cells_y, index * 8 % cells_y
         pencil = index * 8 + lax.broadcasted_iota(jnp.int32, (8, slots), 0)
         calm = scale - scale * jnp.sum((wanted == pencil).astype(F32), axis=1, keepdims=True)
         for begin in range(0, cells_z, LANES):
             wide = slice(begin, begin + LANES)
-            parts = [cells[v, at, wide] for v in range(VARIABLES)]
+            parts = [u_ref[v, x, y : y + 8, wide] for v in range(VARIABLES)]
             inverse, pressure = state_of(parts)
             state_ref[0, at, wide] = parts[SPECIES + 1] * (inverse * scale)
             state_ref[1, at, wide] = parts[SPECIES + 2] * (inverse * calm)
@@ -240,9 +211,8 @@
             state_ref[3, at, wide] = pressure * calm
         return carry
 
-    for x in range(cells_x):
-        incoming[x].wait()
-        lax.fori_loop(x * cells_y // 8, (x + 1) * cells_y // 8, state, 0, unroll=True)
+    for index in range(total // 8):
+        state(index, 0)
 
     pltpu.make_async_copy(pencils, pencils, picked_sem).wait()
     for v in range(VARIABLES):
@@ -382,7 +352,6 @@
     vmem = pltpu.VMEM
     work = vmem((2, span + 8, slots), F32)
     scratch = [
-        vmem((VARIABLES, total, cells_z), F32),
         vmem((VARIABLES, slots, cells_z), F32),
         vmem((VARIABLES, span, slots), F32),
         vmem((span, slots), F32),
@@ -396,14 +365,10 @@
         work,
         vmem((VARIABLES, cells_z + 8, slots), F32),
         vmem((LANES, total), F32),
-        vmem((total, LANES), F32),
-        pltpu.SemaphoreType.DMA(()),
-        pltpu.SemaphoreType.DMA((cells_x,)),
         pltpu.SemaphoreType.DMA(()),
     ]
     smem = pl.BlockSpec(memory_space=pltpu.SMEM)
     whole = pl.BlockSpec(memory_space=pltpu.VMEM)
-    anywhere = pl.BlockSpec(memory_space=pl.ANY)
     return pl.pallas_call(
         shock_kernel,
         out_shape=[
@@ -412,142 +377,135 @@
             jax.ShapeDtypeStruct((total, LANES), F32),
             jax.ShapeDtypeStruct((4, total, cells_z), F32),
         ],
-        in_specs=[smem, smem, anywhere, anywhere, whole, whole, whole],
+        in_specs=[smem, smem, whole, whole, whole, whole, whole],
         out_specs=[whole] * 4,
         scratch_shapes=scratch,
-        compiler_params=pltpu.CompilerParams(vmem_limit_bytes=48 << 20),
+        compiler_params=pltpu.CompilerParams(vmem_limit_bytes=24 << 20),
         cost_estimate=pl.CostEstimate(flops=6_000_000_000, bytes_accessed=14_000_000, transcendentals=4_000_000),
         name="shock",
     )(listed, count, conserved, face, char_left, char_right, listed.reshape(1, slots))
 
 
 def advance_kernel(
-    u_ref, change_ref, hot_ref, edge_ref, state_ref, before_ref, after_ref, out_ref, fluxes, along_y, around, band
+    u_ref,
+    change_ref,
+    hot_ref,
+    edge_ref,
+    state_ref,
+    before_ref,
+    after_ref,
+    out_ref,
+    done,
+    fluxes,
+    along_y,
+    around,
+    band,
+    out_sem,
 ):
-    total, cells_z = u_ref.shape[1], u_ref.shape[2]
+    _, total, cells_z = u_ref.shape
     cells_x = before_ref.shape[2]
     cells_y = total // cells_x
     pitch = cells_y + 16
-    v = pl.program_id(0)
+    halves = cells_z // LANES
     scale = time_step / 60.0
-    normal_y = v == SPECIES + 1
-    normal_z = v == SPECIES + 2
-    energy = v == SPECIES + 3
-
-    @pl.when(v == 0)
-    def _():
-        row = lax.broadcasted_iota(jnp.int32, (cells_z, cells_z), 0)
-        column = lax.broadcasted_iota(jnp.int32, (cells_z, cells_z), 1)
-        weights = stencil(row - column).astype(BF16)
-        band[:cells_z, :] = weights
-        band[cells_z:, :] = weights
+
+    row = lax.broadcasted_iota(jnp.int32, (cells_z, cells_z), 0)
+    column = lax.broadcasted_iota(jnp.int32, (cells_z, cells_z), 1)
+    weights = stencil(row - column).astype(BF16)
+    band[:cells_z, :] = weights
+    band[cells_z:, :] = weights
+    for side, source in enumerate((before_ref, after_ref)):
+        for j in range(WIDTH):
+            for half in range(halves):
+                wide = slice(half * LANES, half * LANES + LANES)
+                parts = [source[j, i, :, wide] for i in range(VARIABLES)]
+                inverse, pressure = state_of(parts)
+                around[side, j, 0, :, wide] = parts[SPECIES + 1] * (inverse * scale)
+                around[side, j, 1, :, wide] = pressure
+
+    lane = lax.broadcasted_iota(jnp.int32, (GROUP, LANES), 1)
+    rows = min(total, 256)
+    for v in range(VARIABLES):
+        turn = v % 2
+
+        def flux_y(value, speed, pressure):
+            if v == SPECIES + 1:
+                return value * speed + scale * pressure
+            if v == SPECIES + 3:
+                return (value + pressure) * speed
+            return value * speed
+
+        def flux_z(value, at, wide):
+            if v == SPECIES + 2:
+                return value * state_ref[1, at, wide] + state_ref[3, at, wide]
+            if v == SPECIES + 3:
+                return (value + state_ref[2, at, wide]) * state_ref[1, at, wide]
+            return value * state_ref[1, at, wide]
+
         for side, source in enumerate((before_ref, after_ref)):
             for j in range(WIDTH):
-                for begin in range(0, cells_z, LANES):
-                    wide = slice(begin, begin + LANES)
-                    parts = [source[j, i, :, wide] for i in range(VARIABLES)]
-                    inverse, pressure = state_of(parts)
-                    around[side, j, 0, :, wide] = parts[SPECIES + 1] * (inverse * scale)
-                    around[side, j, 1, :, wide] = pressure
-
-    def fill(extra_y, extra_z):
-        for side, source in enumerate((before_ref, after_ref)):
-            for j in range(WIDTH):
-                for half in range(cells_z // LANES):
+                begin = 8 - WIDTH + j if side == 0 else 8 + cells_y + j
+                for half in range(halves):
                     wide = slice(half * LANES, half * LANES + LANES)
-                    value = source[j, v, :, wide]
-                    value = extra_y(value, around[side, j, 0, :, wide], around[side, j, 1, :, wide])
-                    begin = 8 - WIDTH + j if side == 0 else 8 + cells_y + j
-                    along_y[half, pl.ds(begin, cells_x, stride=pitch), :] = value
+                    along_y[turn, half, pl.ds(begin, cells_x, stride=pitch), :] = flux_y(
+                        source[j, v, :, wide], around[side, j, 0, :, wide], around[side, j, 1, :, wide]
+                    )
         for begin in range(0, total, GROUP):
             at = slice(begin, begin + GROUP)
             place = begin // cells_y * pitch + 8 + begin % cells_y
-            for half in range(cells_z // LANES):
+            for half in range(halves):
                 wide = slice(half * LANES, half * LANES + LANES)
-                value = u_ref[0, at, wide]
-                along_y[half, place : place + GROUP, :] = extra_y(value, state_ref[0, at, wide], state_ref[2, at, wide])
-                high, low = split(extra_z(value, state_ref[1, at, wide], at, wide))
-                fluxes[at, half * LANES : half * LANES + LANES] = high
-                fluxes[at, cells_z + half * LANES : cells_z + half * LANES + LANES] = low
-
-    plain_y = lambda value, speed, pressure: value * speed
-    plain_z = lambda value, speed, at, wide: value * speed
-
-    @pl.when(jnp.logical_not(normal_y | normal_z | energy))
-    def _():
-        fill(plain_y, plain_z)
-
-    @pl.when(normal_y)
-    def _():
-        fill(lambda value, speed, pressure: value * speed + scale * pressure, plain_z)
-
-    @pl.when(normal_z)
-    def _():
-        fill(plain_y, lambda value, speed, at, wide: value * speed + state_ref[3, at, wide])
-
-    @pl.when(energy)
-    def _():
-        fill(
-            lambda value, speed, pressure: (value + pressure) * speed,
-            lambda value, speed, at, wide: (value + state_ref[2, at, wide]) * speed,
-        )
-
-    lane = lax.broadcasted_iota(jnp.int32, (GROUP, LANES), 1)
-    turn = (LANES - WIDTH - 8 * v) & (LANES - 1)
-    rows = min(total, 256)
-    for base in range(0, total, rows):
-        gained = dot(fluxes[base : base + rows, :], band[...])
-        gained = gained + lax.dot_general(
-            hot_ref[base : base + rows, :], change_ref[0], (((1,), (1,)), ((), ())), preferred_element_type=F32
-        )
-        for begin in range(base, base + rows, GROUP):
-            at = slice(begin, begin + GROUP)
-            place = begin // cells_y * pitch + 8 + begin % cells_y
-            border = pltpu.roll(edge_ref[at, :], turn, 1)
-            for half in range(cells_z // LANES):
-                wide = slice(half * LANES, half * LANES + LANES)
-
-                def read(offset):
-                    return along_y[half, place + offset : place + offset + GROUP, :]
-
-                value = u_ref[0, at, wide] - gained[begin - base : begin - base + GROUP, wide]
-                value = value - (
-                    45.0 * (read(1) - read(-1)) - 9.0 * (read(2) - read(-2)) + (read(3) - read(-3))
+                value = u_ref[v, at, wide]
+                along_y[turn, half, place : place + GROUP, :] = flux_y(
+                    value, state_ref[0, at, wide], state_ref[2, at, wide]
                 )
-                if half == 0:
-                    value = value - jnp.where(lane < WIDTH, border, 0.0)
-                if half == cells_z // LANES - 1:
-                    value = value - jnp.where(lane >= LANES - WIDTH, border, 0.0)
-                out_ref[0, at, wide] = value
+                high, low = split(flux_z(value, at, wide))
+                fluxes[turn, at, half * LANES : half * LANES + LANES] = high
+                fluxes[turn, at, cells_z + half * LANES : cells_z + half * LANES + LANES] = low
+        for base in range(0, total, rows):
+            gained = dot(fluxes[turn, base : base + rows, :], band[...])
+            gained = gained + lax.dot_general(
+                hot_ref[base : base + rows, :], change_ref[v], (((1,), (1,)), ((), ())), preferred_element_type=F32
+            )
+            for begin in range(base, base + rows, GROUP):
+                at = slice(begin, begin + GROUP)
+                place = begin // cells_y * pitch + 8 + begin % cells_y
+                border = pltpu.roll(edge_ref[at, :], (LANES - WIDTH - 8 * v) % LANES, 1)
+                for half in range(halves):
+                    wide = slice(half * LANES, half * LANES + LANES)
+
+                    def read(offset):
+                        return along_y[turn, half, place + offset : place + offset + GROUP, :]
+
+                    value = u_ref[v, at, wide] - gained[begin - base : begin - base + GROUP, wide]
+                    value = value - (
+                        45.0 * (read(1) - read(-1)) - 9.0 * (read(2) - read(-2)) + (read(3) - read(-3))
+                    )
+                    if half == 0:
+                        value = value - jnp.where(lane < WIDTH, border, 0.0)
+                    if half == halves - 1:
+                        value = value - jnp.where(lane >= LANES - WIDTH, border, 0.0)
+                    done[v, at, wide] = value
+        pltpu.make_async_copy(done.at[v], out_ref.at[v], out_sem).start()
+    pltpu.make_async_copy(done, done, out_sem).wait()
 
 
 def advance(conserved, change, hot, edge, state, before, after):
     _, cells_x, cells_y, cells_z = conserved.shape
     total = cells_x * cells_y
-    one = pl.BlockSpec((1, total, cells_z), lambda v: (v, 0, 0))
-
-    def fixed(array):
-        return pl.BlockSpec(array.shape, lambda v: (0,) * array.ndim)
-
+    whole = pl.BlockSpec(memory_space=pltpu.VMEM)
     result = pl.pallas_call(
         advance_kernel,
         out_shape=jax.ShapeDtypeStruct((VARIABLES, total, cells_z), F32),
-        grid=(VARIABLES,),
-        in_specs=[
-            one,
-            pl.BlockSpec((1,) + change.shape[1:], lambda v: (v, 0, 0)),
-            fixed(hot),
-            fixed(edge),
-            fixed(state),
-            fixed(before),
-            fixed(after),
-        ],
-        out_specs=one,
+        in_specs=[whole] * 7,
+        out_specs=pl.BlockSpec(memory_space=pl.ANY),
         scratch_shapes=[
-            pltpu.VMEM((total, 2 * cells_z), BF16),
-            pltpu.VMEM((cells_z // LANES, cells_x * (cells_y + 16), LANES), F32),
+            pltpu.VMEM((VARIABLES, total, cells_z), F32),
+            pltpu.VMEM((2, total, 2 * cells_z), BF16),
+            pltpu.VMEM((2, cells_z // LANES, cells_x * (cells_y + 16), LANES), F32),
             pltpu.VMEM((2, WIDTH, 2, cells_x, cells_z), F32),
             pltpu.VMEM((2 * cells_z, cells_z), BF16),
+            pltpu.SemaphoreType.DMA(()),
         ],
         compiler_params=pltpu.CompilerParams(vmem_limit_bytes=24 << 20),
         cost_estimate=pl.CostEstimate(flops=4_000_000_000, bytes_accessed=20_000_000, transcendentals=0),
@@ -560,10 +518,10 @@
     slots = shock_list.shape[-1]
     count = lax.axis_size("gy")
     ahead = [(i, (i + 1) % count) for i in range(count)]
-    tail, head = pack_y(conserved)
+    tail, head, packed = pack(conserved)
     before = lax.ppermute(tail, "gy", ahead)
     after = lax.ppermute(head, "gy", [(b, a) for a, b in ahead])
-    face = exchange_z(pack_z(conserved))
+    face = exchange_z(packed)
     change, hot, edge, state = shock(
         shock_list.reshape(slots), shock_count.reshape(1), conserved, face, char_left, char_right
     )

time: 41.6 us -> 35.5 us (0.85)
  Pallas kernels: 35.4 us -> 25.3 us
  local copies, waits for them, and re-layouts: 0.02 us -> 3.79 us
    pallas_call x2 -> x1, Pallas kernels: 9.05 us -> 1.53 us  [pack(): pl.pallas_call(pack_kernel, out_shape=[rows, rows, jax.ShapeDtypeStruct((...]
    unnamed x10, local copies, waits for them, and re-layouts: 0.02 us -> 3.79 us
    pallas_call x1, Pallas kernels: 11.3 us -> 9.39 us  [advance(): pl.pallas_call(advance_kernel, out_shape=jax.ShapeDtypeStruct((VARIABLES,...]
    pallas_call x1, Pallas kernels: 15 us -> 14.4 us  [shock(): pl.pallas_call(shock_kernel, out_shape=[jax.ShapeDtypeStruct((VARIABLES,...]
where the time goes in v2:
time: 35.5 us; the launch traced here: 35.3 us
  Pallas kernels  25.3 us (71%)
  starting transfers between devices  5.27 us (15%)
  local copies, waits for them, and re-layouts  3.79 us (11%)
  between operations  0.89 us (3%)
    pallas_call x1, Pallas kernels, shock(): pl.pallas_call(shock_kernel, out_shape=[jax.ShapeDtypeStruct((VARIABLES,...  14.4 us
    pallas_call x1, Pallas kernels, advance(): pl.pallas_call(advance_kernel, out_shape=jax.ShapeDtypeStruct((VARIABLES,...  9.39 us
    unnamed x10, local copies, waits for them, and re-layouts  3.79 us
    ppermute x1, starting transfers between devices, on_device(): before = lax.ppermute(tail, 'gy', ahead)  2.64 us
    ppermute x1, starting transfers between devices, on_device(): after = lax.ppermute(head, 'gy', [(b, a) for a, b in ahead])  2.11 us
    pallas_call x1, Pallas kernels, pack(): pl.pallas_call(pack_kernel, out_shape=[rows, rows, jax.ShapeDtypeStruct((...  1.53 us
  transfers between devices with their start and end apart: 3, of which 0 were waited for; matrix products, arithmetic and copies ran while one was open for 0% of the time, Pallas kernels for 41%

profile of v2, /device:TPU:0, one launch (start us, length us, event | category | flops | bytes accessed | tf_op | source)
XLA Modules:
  0.0 35.3 jit_solution(11064050473164807300)
XLA Ops:
  0.0 0.0 copy-start
  0.0 3.1 %copy-done = f32[14,8,64,256]{3,2,1,0:T(8,128)S(1)} copy-done((f32[14,8,64,256]{3,2,1,0:T(8,128)S(1)}, f32[14,8,64,256]{3,2,1,0:T(8,128)}, u32[]{:S(2)}) %copy-start) | copy-done | bytes 7340056
  3.1 0.0 copy-start.1
  3.1 0.0 copy-start.2
  3.1 0.0 copy-start.4
  3.1 1.5 %pack.1 = (f32[3,14,8,256]{3,2,1,0:T(8,128)S(1)}, f32[3,14,8,256]{3,2,1,0:T(8,128)S(1)}, f32[512,128]{1,0:T(8,128)S(1)}) custom-call(f32[14,8,64,256]{3,2,1,0:T(8,128)S(1)} %copy-done), custom_call_target="tpu_custom_call" | custom-call | flops 4000000 | bytes 9000000 | tf_op jit(solution)/shard_map/pack/pallas_call | solution.py:79
  4.6 0.5 %collective-permute-start = (f32[512,128]{1,0:T(8,128)S(1)}, f32[512,128]{1,0:T(8,128)S(1)}, u32[]{:S(2)}, u32[]{:S(2)}) collective-permute-start(f32[512,128]{1,0:T(8,128)S(1)} %get-tuple-element.12), channel_id=1, source_target_pairs={{0,1},{1,0},{2,3},{3,2},{4,5},{5,4},{6,7},{7,6},{8,9},{9,8},{10,11... | collective-permute-start | bytes 786440 | tf_op jit(solution)/shard_map/ppermute | solution.py:96
  5.1 2.6 %collective-permute-start.1 = (f32[3,14,8,256]{3,2,1,0:T(8,128)S(1)}, f32[3,14,8,256]{3,2,1,0:T(8,128)S(1)}, u32[]{:S(2)}, u32[]{:S(2)}) collective-permute-start(f32[3,14,8,256]{3,2,1,0:T(8,128)S(1)} %get-tuple-element.17), channel_id=1, source_target_pairs={{0,2},{2,4},{4,6},{6,0},{1,3},{3,5},{5,7},{7,1},{8,10},{10,12},{12... | collective-permute-start | bytes 1032200 | tf_op jit(solution)/shard_map/ppermute | solution.py:522
  7.8 2.1 %collective-permute-start.2 = (f32[3,14,8,256]{3,2,1,0:T(8,128)S(1)}, f32[3,14,8,256]{3,2,1,0:T(8,128)S(1)}, u32[]{:S(2)}, u32[]{:S(2)}) collective-permute-start(f32[3,14,8,256]{3,2,1,0:T(8,128)S(1)} %get-tuple-element.18), channel_id=1, source_target_pairs={{2,0},{4,2},{6,4},{0,6},{3,1},{5,3},{7,5},{1,7},{10,8},{12,10},{14... | collective-permute-start | bytes 1032200 | tf_op jit(solution)/shard_map/ppermute | solution.py:523
  10.5 0.0 collective-permute-done.face_ref
  10.6 0.0 copy-done.1
  10.6 0.0 copy-done.2
  10.6 0.0 copy-done.4
  10.6 0.0 copy-start.3
  10.6 0.7 %copy-done.3 = f32[14,14]{1,0:T(8,128)S(1)} copy-done((f32[14,14]{1,0:T(8,128)S(1)}, f32[14,14]{1,0:T(8,128)}, u32[]{:S(2)}) %copy-start.3) | copy-done | bytes 808
  11.3 14.4 %shock.1 = (bf16[14,256,256]{2,1,0:T(8,128)(2,1)S(1)}, bf16[512,256]{1,0:T(8,128)(2,1)S(1)}, f32[512,128]{1,0:T(8,128)S(1)}, f32[4,512,256]{2,1,0:T(8,128)S(1)}) custom-call(s32[128]{0:T(128)S(1)} %bitcast.7, s32[1]{0:T(128)} %bitcast.5.count_ref, f32[14,8,64,256]{3,2,1,0:T(8,128)S(1)} %copy-done.1, f32[512,128]{1,0:T(8,128)S(1)} %collective-permute-done.face_ref, ...), custom_call_target="tpu_custom_call" | custom-call | flops 6000000000 | bytes 14000000 | tf_op jit(solution)/shard_map/shock/pallas_call | solution.py:372
  25.7 0.0 collective-permute-done.1.before_ref
  25.7 0.0 collective-permute-done.2.after_ref
  25.7 9.4 %advance.1 = f32[14,512,256]{2,1,0:T(8,128)} custom-call(f32[14,512,256]{2,1,0:T(8,128)S(1)} %bitcast.6, bf16[14,256,256]{2,1,0:T(8,128)(2,1)S(1)} %get-tuple-element.13.change_ref, bf16[512,256]{1,0:T(8,128)(2,1)S(1)} %get-tuple-element.14.hot_ref, f32[512,128]{1,0:T(8,128)S(1)} %get-tuple-element.15.edge_ref, ...), custom_call_target="tpu_custom_call" | custom-call | flops 4000000000 | bytes 20000000 | tf_op jit(solution)/shard_map/advance/pallas_call | solution.py:497
Async XLA Ops:
  0.0 3.1 %copy-start = (f32[14,8,64,256]{3,2,1,0:T(8,128)S(1)}, f32[14,8,64,256]{3,2,1,0:T(8,128)}, u32[]{:S(2)}) copy-start(f32[14,8,64,256]{3,2,1,0:T(8,128)} %u_ref.3) | copy-start | bytes 22020100
  3.1 7.5 %copy-start.1 = (f32[14,8,64,256]{3,2,1,0:T(8,128)S(1)}, f32[14,8,64,256]{3,2,1,0:T(8,128)}, u32[]{:S(2)}) copy-start(f32[14,8,64,256]{3,2,1,0:T(8,128)} %u_ref.3) | copy-start | bytes 22020100
  3.1 7.5 %copy-start.2 = (f32[14,14]{1,0:T(8,128)S(1)}, f32[14,14]{1,0:T(8,128)}, u32[]{:S(2)}) copy-start(f32[14,14]{1,0:T(8,128)} %left_ref.1) | copy-start | bytes 2356
  3.1 7.5 %copy-start.4 = (s32[1,1,1,128]{3,2,1,0:T(1,128)S(1)}, s32[1,1,1,128]{3,2,1,0:T(1,128)}, u32[]{:S(2)}) copy-start(s32[1,1,1,128]{3,2,1,0:T(1,128)} %param.8) | copy-start | bytes 1540
  4.6 5.9 %collective-permute-start = (f32[512,128]{1,0:T(8,128)S(1)}, f32[512,128]{1,0:T(8,128)S(1)}, u32[]{:S(2)}, u32[]{:S(2)}) collective-permute-start(f32[512,128]{1,0:T(8,128)S(1)} %get-tuple-element.12), channel_id=1, source_target_pairs={{0,1},{1,0},{2,3},{3,2},{4,5},{5,4},{6,7},{7,6},{8,9},{9,8},{10,11... | collective-permute-start | bytes 786440 | tf_op jit(solution)/shard_map/ppermute | solution.py:96
  5.1 20.6 %collective-permute-start.1 = (f32[3,14,8,256]{3,2,1,0:T(8,128)S(1)}, f32[3,14,8,256]{3,2,1,0:T(8,128)S(1)}, u32[]{:S(2)}, u32[]{:S(2)}) collective-permute-start(f32[3,14,8,256]{3,2,1,0:T(8,128)S(1)} %get-tuple-element.17), channel_id=1, source_target_pairs={{0,2},{2,4},{4,6},{6,0},{1,3},{3,5},{5,7},{7,1},{8,10},{10,12},{12... | collective-permute-start | bytes 1032200 | tf_op jit(solution)/shard_map/ppermute | solution.py:522
  7.8 18.0 %collective-permute-start.2 = (f32[3,14,8,256]{3,2,1,0:T(8,128)S(1)}, f32[3,14,8,256]{3,2,1,0:T(8,128)S(1)}, u32[]{:S(2)}, u32[]{:S(2)}) collective-permute-start(f32[3,14,8,256]{3,2,1,0:T(8,128)S(1)} %get-tuple-element.18), channel_id=1, source_target_pairs={{2,0},{4,2},{6,4},{0,6},{3,1},{5,3},{7,5},{1,7},{10,8},{12,10},{14... | collective-permute-start | bytes 1032200 | tf_op jit(solution)/shard_map/ppermute | solution.py:523
  10.6 0.7 %copy-start.3 = (f32[14,14]{1,0:T(8,128)S(1)}, f32[14,14]{1,0:T(8,128)}, u32[]{:S(2)}) copy-start(f32[14,14]{1,0:T(8,128)} %right_ref.1) | copy-start | bytes 2356

commit v3 on v2

--- a/solution.py
+++ b/solution.py
@@ -78,7 +78,11 @@
     rows = jax.ShapeDtypeStruct((WIDTH, VARIABLES, cells_x, cells_z), F32)
     return pl.pallas_call(
         pack_kernel,
-        out_shape=[rows, rows, jax.ShapeDtypeStruct((cells_x * cells_y, LANES), F32)],
+        out_shape=[
+            rows,
+            rows,
+            jax.ShapeDtypeStruct((cells_x * cells_y, LANES), F32),
+        ],
         in_specs=[pl.BlockSpec(memory_space=pltpu.VMEM)],
         out_specs=[pl.BlockSpec(memory_space=pltpu.VMEM)] * 3,
         scratch_shapes=[pltpu.SemaphoreType.DMA(())],
@@ -145,26 +149,22 @@
     third,
     faces,
     edge_t,
-    picked_sem,
 ):
     _, cells_x, cells_y, cells_z = u_ref.shape
-    slots = row_ref.shape[1]
+    slots = row_ref.shape[-1]
     total = cells_x * cells_y
     span = turned.shape[1]
 
-    def fetch(p, carry):
-        place = list_ref[p]
-        pltpu.make_async_copy(
-            u_ref.at[:, place // cells_y, pl.ds(place % cells_y, 1), :], pencils.at[:, pl.ds(p, 1), :], picked_sem
-        ).start()
-        return carry
-
-    lax.fori_loop(0, slots, fetch, 0)
-    left_high, left_low = spread_matrix(0.5 * left_ref[...])
-    right_high, right_low = spread_matrix((time_step / 3.0) * right_ref[...])
-    live = count_ref[0]
+    def fetch(p):
+        place = list_ref[0, 0, 0, p]
+        x, y = place // cells_y, place % cells_y
+        for v in range(VARIABLES):
+            pencils[v, pl.ds(p, 1), :] = u_ref[v, x, pl.ds(y, 1), :]
+
+
+    live = count_ref[0, 0, 0]
     lane_slots = lax.broadcasted_iota(jnp.int32, (1, slots), 1)
-    wanted = jnp.where(lane_slots < live, row_ref[...], -1)
+    wanted = jnp.where(lane_slots < live, row_ref[0, 0], -1)
     scale = time_step / 60.0
 
     for begin in range(0, total, LANES):
@@ -189,8 +189,11 @@
         hot_ref[wide, :slots] = hot
         hot_ref[wide, slots:] = hot
 
+    left_high, left_low = spread_matrix(0.5 * left_ref[...])
+    right_high, right_low = spread_matrix((time_step / 3.0) * right_ref[...])
+
     def neighbour(p, carry):
-        speed_t[pl.ds(p, 1), :] = face_ref[pl.ds(list_ref[p], 1), :]
+        speed_t[pl.ds(p, 1), :] = face_ref[pl.ds(list_ref[0, 0, 0, p], 1), :]
         return carry
 
     lax.fori_loop(0, slots, neighbour, 0, unroll=8)
@@ -213,8 +216,9 @@
 
     for index in range(total // 8):
         state(index, 0)
-
-    pltpu.make_async_copy(pencils, pencils, picked_sem).wait()
+        for p in range(index * 8 * slots // total, (index + 1) * 8 * slots // total):
+            fetch(p)
+
     for v in range(VARIABLES):
         tile = border[8 * v : 8 * v + 8, :]
         turned[v, 0:LEAD, :] = tile
@@ -346,7 +350,7 @@
 
 def shock(listed, count, conserved, face, char_left, char_right):
     _, cells_x, cells_y, cells_z = conserved.shape
-    slots = listed.shape[0]
+    slots = listed.shape[-1]
     total = cells_x * cells_y
     span = -(-(cells_z + 2 * LEAD) // GROUP) * GROUP
     vmem = pltpu.VMEM
@@ -365,7 +369,6 @@
         work,
         vmem((VARIABLES, cells_z + 8, slots), F32),
         vmem((LANES, total), F32),
-        pltpu.SemaphoreType.DMA(()),
     ]
     smem = pl.BlockSpec(memory_space=pltpu.SMEM)
     whole = pl.BlockSpec(memory_space=pltpu.VMEM)
@@ -383,108 +386,89 @@
         compiler_params=pltpu.CompilerParams(vmem_limit_bytes=24 << 20),
         cost_estimate=pl.CostEstimate(flops=6_000_000_000, bytes_accessed=14_000_000, transcendentals=4_000_000),
         name="shock",
-    )(listed, count, conserved, face, char_left, char_right, listed.reshape(1, slots))
+    )(listed, count, conserved, face, char_left, char_right, listed)
 
 
 def advance_kernel(
-    u_ref,
-    change_ref,
-    hot_ref,
-    edge_ref,
-    state_ref,
-    before_ref,
-    after_ref,
-    out_ref,
-    done,
-    fluxes,
-    along_y,
-    around,
-    band,
-    out_sem,
+    u_ref, change_ref, hot_ref, edge_ref, state_ref, before_ref, after_ref, out_ref, done, left, right, rim, out_sem
 ):
     _, total, cells_z = u_ref.shape
     cells_x = before_ref.shape[2]
     cells_y = total // cells_x
-    pitch = cells_y + 16
     halves = cells_z // LANES
     scale = time_step / 60.0
+    rows = right.shape[2] // 2 - cells_z
 
     row = lax.broadcasted_iota(jnp.int32, (cells_z, cells_z), 0)
     column = lax.broadcasted_iota(jnp.int32, (cells_z, cells_z), 1)
-    weights = stencil(row - column).astype(BF16)
-    band[:cells_z, :] = weights
-    band[cells_z:, :] = weights
-    for side, source in enumerate((before_ref, after_ref)):
-        for j in range(WIDTH):
-            for half in range(halves):
-                wide = slice(half * LANES, half * LANES + LANES)
-                parts = [source[j, i, :, wide] for i in range(VARIABLES)]
-                inverse, pressure = state_of(parts)
-                around[side, j, 0, :, wide] = parts[SPECIES + 1] * (inverse * scale)
-                around[side, j, 1, :, wide] = pressure
+    along_z = stencil(row - column).astype(BF16)
+    row = lax.broadcasted_iota(jnp.int32, (rows, rows), 0)
+    column = lax.broadcasted_iota(jnp.int32, (rows, rows), 1)
+    inside = row // cells_y == column // cells_y
+    along_y = jnp.where(inside, stencil(column - row), 0.0).astype(BF16)
+    for turn in range(2):
+        for block in range(total // rows):
+            for k in range(2):
+                left[turn, block, :, 2 * cells_z + k * rows : 2 * cells_z + k * rows + rows] = along_y
+                right[turn, block, k * cells_z : k * cells_z + cells_z, :] = along_z
+
+    rim[...] = jnp.zeros_like(rim)
+    for half in range(halves):
+        wide = slice(half * LANES, half * LANES + LANES)
+        f0, f1, f2 = (flux_of([before_ref[j, v, :, wide] for v in range(VARIABLES)], 1) for j in range(WIDTH))
+        for v in range(VARIABLES):
+            for j, part in enumerate((45.0 * f2[v] - 9.0 * f1[v] + f0[v], f1[v] - 9.0 * f2[v], f2[v])):
+                rim[v, half, pl.ds(j, cells_x, stride=2 * GROUP), :] = scale * part
+        f0, f1, f2 = (flux_of([after_ref[j, v, :, wide] for v in range(VARIABLES)], 1) for j in range(WIDTH))
+        for v in range(VARIABLES):
+            for j, part in enumerate((f0[v], f1[v] - 9.0 * f0[v], 45.0 * f0[v] - 9.0 * f1[v] + f2[v])):
+                rim[v, half, pl.ds(2 * GROUP - WIDTH + j, cells_x, stride=2 * GROUP), :] = -scale * part
 
     lane = lax.broadcasted_iota(jnp.int32, (GROUP, LANES), 1)
-    rows = min(total, 256)
     for v in range(VARIABLES):
         turn = v % 2
 
-        def flux_y(value, speed, pressure):
-            if v == SPECIES + 1:
-                return value * speed + scale * pressure
-            if v == SPECIES + 3:
-                return (value + pressure) * speed
-            return value * speed
-
-        def flux_z(value, at, wide):
-            if v == SPECIES + 2:
-                return value * state_ref[1, at, wide] + state_ref[3, at, wide]
-            if v == SPECIES + 3:
-                return (value + state_ref[2, at, wide]) * state_ref[1, at, wide]
-            return value * state_ref[1, at, wide]
-
-        for side, source in enumerate((before_ref, after_ref)):
-            for j in range(WIDTH):
-                begin = 8 - WIDTH + j if side == 0 else 8 + cells_y + j
-                for half in range(halves):
-                    wide = slice(half * LANES, half * LANES + LANES)
-                    along_y[turn, half, pl.ds(begin, cells_x, stride=pitch), :] = flux_y(
-                        source[j, v, :, wide], around[side, j, 0, :, wide], around[side, j, 1, :, wide]
-                    )
         for begin in range(0, total, GROUP):
             at = slice(begin, begin + GROUP)
-            place = begin // cells_y * pitch + 8 + begin % cells_y
-            for half in range(halves):
-                wide = slice(half * LANES, half * LANES + LANES)
-                value = u_ref[v, at, wide]
-                along_y[turn, half, place : place + GROUP, :] = flux_y(
-                    value, state_ref[0, at, wide], state_ref[2, at, wide]
-                )
-                high, low = split(flux_z(value, at, wide))
-                fluxes[turn, at, half * LANES : half * LANES + LANES] = high
-                fluxes[turn, at, cells_z + half * LANES : cells_z + half * LANES + LANES] = low
-        for base in range(0, total, rows):
-            gained = dot(fluxes[turn, base : base + rows, :], band[...])
+            block, place = begin // rows, begin % rows
+            value = u_ref[v, at, :]
+            flux_y = value * state_ref[0, at, :]
+            flux_z = value * state_ref[1, at, :]
+            if v == SPECIES + 1:
+                flux_y = flux_y + scale * state_ref[2, at, :]
+            if v == SPECIES + 2:
+                flux_z = flux_z + state_ref[3, at, :]
+            if v == SPECIES + 3:
+                flux_y = flux_y + state_ref[2, at, :] * state_ref[0, at, :]
+                flux_z = flux_z + state_ref[2, at, :] * state_ref[1, at, :]
+            high, low = split(flux_z)
+            left[turn, block, place : place + GROUP, :cells_z] = high
+            left[turn, block, place : place + GROUP, cells_z : 2 * cells_z] = low
+            high, low = split(flux_y)
+            place = place + 2 * cells_z
+            right[turn, block, place : place + GROUP, :] = high
+            right[turn, block, place + rows : place + rows + GROUP, :] = low
+        for block in range(total // rows):
+            base = block * rows
+            gained = dot(left[turn, block], right[turn, block])
             gained = gained + lax.dot_general(
                 hot_ref[base : base + rows, :], change_ref[v], (((1,), (1,)), ((), ())), preferred_element_type=F32
             )
             for begin in range(base, base + rows, GROUP):
                 at = slice(begin, begin + GROUP)
-                place = begin // cells_y * pitch + 8 + begin % cells_y
+                x, y = begin // cells_y, begin % cells_y
                 border = pltpu.roll(edge_ref[at, :], (LANES - WIDTH - 8 * v) % LANES, 1)
                 for half in range(halves):
                     wide = slice(half * LANES, half * LANES + LANES)
-
-                    def read(offset):
-                        return along_y[turn, half, place + offset : place + offset + GROUP, :]
-
                     value = u_ref[v, at, wide] - gained[begin - base : begin - base + GROUP, wide]
-                    value = value - (
-                        45.0 * (read(1) - read(-1)) - 9.0 * (read(2) - read(-2)) + (read(3) - read(-3))
-                    )
                     if half == 0:
                         value = value - jnp.where(lane < WIDTH, border, 0.0)
                     if half == halves - 1:
                         value = value - jnp.where(lane >= LANES - WIDTH, border, 0.0)
+                    if y == 0:
+                        value = value + rim[v, half, 2 * GROUP * x : 2 * GROUP * x + GROUP, :]
+                    if y == cells_y - GROUP:
+                        value = value + rim[v, half, 2 * GROUP * x + GROUP : 2 * GROUP * x + 2 * GROUP, :]
                     done[v, at, wide] = value
         pltpu.make_async_copy(done.at[v], out_ref.at[v], out_sem).start()
     pltpu.make_async_copy(done, done, out_sem).wait()
@@ -493,6 +477,7 @@
 def advance(conserved, change, hot, edge, state, before, after):
     _, cells_x, cells_y, cells_z = conserved.shape
     total = cells_x * cells_y
+    rows = cells_y * max(1, min(cells_x, 256 // cells_y))
     whole = pl.BlockSpec(memory_space=pltpu.VMEM)
     result = pl.pallas_call(
         advance_kernel,
@@ -501,10 +486,9 @@
         out_specs=pl.BlockSpec(memory_space=pl.ANY),
         scratch_shapes=[
             pltpu.VMEM((VARIABLES, total, cells_z), F32),
-            pltpu.VMEM((2, total, 2 * cells_z), BF16),
-            pltpu.VMEM((2, cells_z // LANES, cells_x * (cells_y + 16), LANES), F32),
-            pltpu.VMEM((2, WIDTH, 2, cells_x, cells_z), F32),
-            pltpu.VMEM((2 * cells_z, cells_z), BF16),
+            pltpu.VMEM((2, total // rows, rows, 2 * (cells_z + rows)), BF16),
+            pltpu.VMEM((2, total // rows, 2 * (cells_z + rows), cells_z), BF16),
+            pltpu.VMEM((VARIABLES, cells_z // LANES, cells_x * 2 * GROUP, LANES), F32),
             pltpu.SemaphoreType.DMA(()),
         ],
         compiler_params=pltpu.CompilerParams(vmem_limit_bytes=24 << 20),
@@ -515,7 +499,6 @@
 
 
 def on_device(conserved, char_left, char_right, shock_list, shock_count):
-    slots = shock_list.shape[-1]
     count = lax.axis_size("gy")
     ahead = [(i, (i + 1) % count) for i in range(count)]
     tail, head, packed = pack(conserved)
@@ -523,7 +506,7 @@
     after = lax.ppermute(head, "gy", [(b, a) for a, b in ahead])
     face = exchange_z(packed)
     change, hot, edge, state = shock(
-        shock_list.reshape(slots), shock_count.reshape(1), conserved, face, char_left, char_right
+        shock_list, shock_count, conserved, face, char_left, char_right
     )
     return advance(conserved, change, hot, edge, state, before, after)
 

time: 35.5 us -> 33.1 us (0.932)
  Pallas kernels: 25.3 us -> 21.4 us
  waiting for transfers between devices: 0.01 us -> 0.87 us
  local copies, waits for them, and re-layouts: 3.79 us -> 4.48 us
    pallas_call x1, Pallas kernels: 14.4 us -> 12.4 us  [shock(): pl.pallas_call(shock_kernel, out_shape=[jax.ShapeDtypeStruct((VARIABLES,...]
    pallas_call x1, Pallas kernels: 9.39 us -> 7.44 us  [advance(): pl.pallas_call(advance_kernel, out_shape=jax.ShapeDtypeStruct((VARIABLES,...]
    ppermute x1, waiting for transfers between devices: 0.01 us -> 0.87 us  [on_device(): after = lax.ppermute(head, 'gy', [(b, a) for a, b in ahead])]
    unnamed x10, local copies, waits for them, and re-layouts: 3.79 us -> 4.48 us
  transfers between devices with their start and end apart: 3 -> 3, of which waited for: 0 -> 1; matrix products, arithmetic and copies ran while one was open for 0% -> 0% of each run, Pallas kernels for 41% -> 38%
where the time goes in v3:
time: 33.1 us; the launch traced here: 32.9 us
  Pallas kernels  21.4 us (65%)
  starting transfers between devices  5.27 us (16%)
  local copies, waits for them, and re-layouts  4.48 us (14%)
  waiting for transfers between devices  0.87 us (3%)
  between operations  0.87 us (3%)
    pallas_call x1, Pallas kernels, shock(): pl.pallas_call(shock_kernel, out_shape=[jax.ShapeDtypeStruct((VARIABLES,...  12.4 us
    pallas_call x1, Pallas kernels, advance(): pl.pallas_call(advance_kernel, out_shape=jax.ShapeDtypeStruct((VARIABLES,...  7.44 us
    unnamed x10, local copies, waits for them, and re-layouts  4.48 us
    ppermute x1, starting transfers between devices, on_device(): before = lax.ppermute(tail, 'gy', ahead)  2.64 us
    ppermute x1, starting transfers between devices, on_device(): after = lax.ppermute(head, 'gy', [(b, a) for a, b in ahead])  2.11 us
    pallas_call x1, Pallas kernels, pack(): pl.pallas_call(pack_kernel, out_shape=[rows, rows, jax.ShapeDtypeStruct((...  1.53 us
    ppermute x1, waiting for transfers between devices, on_device(): after = lax.ppermute(head, 'gy', [(b, a) for a, b in ahead])  0.87 us
  transfers between devices with their start and end apart: 3, of which 1 were waited for; matrix products, arithmetic and copies ran while one was open for 0% of the time, Pallas kernels for 38%

profile of v3, /device:TPU:0, one launch (start us, length us, event | category | flops | bytes accessed | tf_op | source)
XLA Modules:
  0.0 32.9 jit_solution(13495768724597317055)
XLA Ops:
  0.0 0.0 copy-start
  0.0 3.1 %copy-done = f32[14,8,64,256]{3,2,1,0:T(8,128)S(1)} copy-done((f32[14,8,64,256]{3,2,1,0:T(8,128)S(1)}, f32[14,8,64,256]{3,2,1,0:T(8,128)}, u32[]{:S(2)}) %copy-start) | copy-done | bytes 7340056
  3.1 0.0 copy-start.1
  3.1 0.0 copy-start.4
  3.1 1.5 %pack.1 = (f32[3,14,8,256]{3,2,1,0:T(8,128)S(1)}, f32[3,14,8,256]{3,2,1,0:T(8,128)S(1)}, f32[512,128]{1,0:T(8,128)S(1)}) custom-call(f32[14,8,64,256]{3,2,1,0:T(8,128)S(1)} %copy-done), custom_call_target="tpu_custom_call" | custom-call | flops 4000000 | bytes 9000000 | tf_op jit(solution)/shard_map/pack/pallas_call | solution.py:79
  4.6 0.5 %collective-permute-start = (f32[512,128]{1,0:T(8,128)S(1)}, f32[512,128]{1,0:T(8,128)S(1)}, u32[]{:S(2)}, u32[]{:S(2)}) collective-permute-start(f32[512,128]{1,0:T(8,128)S(1)} %get-tuple-element.12), channel_id=1, source_target_pairs={{0,1},{1,0},{2,3},{3,2},{4,5},{5,4},{6,7},{7,6},{8,9},{9,8},{10,11... | collective-permute-start | bytes 786440 | tf_op jit(solution)/shard_map/ppermute | solution.py:100
  5.1 2.6 %collective-permute-start.1 = (f32[3,14,8,256]{3,2,1,0:T(8,128)S(1)}, f32[3,14,8,256]{3,2,1,0:T(8,128)S(1)}, u32[]{:S(2)}, u32[]{:S(2)}) collective-permute-start(f32[3,14,8,256]{3,2,1,0:T(8,128)S(1)} %get-tuple-element.17), channel_id=1, source_target_pairs={{0,2},{2,4},{4,6},{6,0},{1,3},{3,5},{5,7},{7,1},{8,10},{10,12},{12... | collective-permute-start | bytes 1032200 | tf_op jit(solution)/shard_map/ppermute | solution.py:505
  7.8 2.1 %collective-permute-start.2 = (f32[3,14,8,256]{3,2,1,0:T(8,128)S(1)}, f32[3,14,8,256]{3,2,1,0:T(8,128)S(1)}, u32[]{:S(2)}, u32[]{:S(2)}) collective-permute-start(f32[3,14,8,256]{3,2,1,0:T(8,128)S(1)} %get-tuple-element.18), channel_id=1, source_target_pairs={{2,0},{4,2},{6,4},{0,6},{3,1},{5,3},{7,5},{1,7},{10,8},{12,10},{14... | collective-permute-start | bytes 1032200 | tf_op jit(solution)/shard_map/ppermute | solution.py:506
  10.5 0.0 collective-permute-done.face_ref
  10.6 0.0 copy-done.1
  10.6 0.0 copy-done.4
  10.6 0.0 copy-start.2
  10.6 0.7 %copy-done.2 = f32[14,14]{1,0:T(8,128)S(1)} copy-done((f32[14,14]{1,0:T(8,128)S(1)}, f32[14,14]{1,0:T(8,128)}, u32[]{:S(2)}) %copy-start.2) | copy-done | bytes 808
  11.3 0.0 copy-start.3
  11.3 0.7 %copy-done.3 = f32[14,14]{1,0:T(8,128)S(1)} copy-done((f32[14,14]{1,0:T(8,128)S(1)}, f32[14,14]{1,0:T(8,128)}, u32[]{:S(2)}) %copy-start.3) | copy-done | bytes 808
  12.0 12.4 %shock.1 = (bf16[14,256,256]{2,1,0:T(8,128)(2,1)S(1)}, bf16[512,256]{1,0:T(8,128)(2,1)S(1)}, f32[512,128]{1,0:T(8,128)S(1)}, f32[4,512,256]{2,1,0:T(8,128)S(1)}) custom-call(s32[1,1,1,128]{3,2,1,0:T(1,128)S(1)} %copy-done.4, s32[1,1,1]{2,1,0:T(1,128)S(6)} %copy.6.count_ref, f32[14,8,64,256]{3,2,1,0:T(8,128)S(1)} %copy-done.1, ...), custom_call_target="tpu_custom_call" | custom-call | flops 6000000000 | bytes 14000000 | tf_op jit(solution)/shard_map/shock/pallas_call | solution.py:375
  24.4 0.0 collective-permute-done.1.before_ref
  24.4 0.9 %collective-permute-done.2.after_ref = f32[3,14,8,256]{3,2,1,0:T(8,128)S(1)} collective-permute-done((f32[3,14,8,256]{3,2,1,0:T(8,128)S(1)}, f32[3,14,8,256]{3,2,1,0:T(8,128)S(1)}, u32[]{:S(2)}, u32[]{:S(2)}) %collective-permute-start.2) | collective-permute-done | bytes 344096 | tf_op jit(solution)/shard_map/ppermute | solution.py:506
  25.3 7.4 %advance.1 = f32[14,512,256]{2,1,0:T(8,128)} custom-call(f32[14,512,256]{2,1,0:T(8,128)S(1)} %bitcast.2, bf16[14,256,256]{2,1,0:T(8,128)(2,1)S(1)} %get-tuple-element.13.change_ref, bf16[512,256]{1,0:T(8,128)(2,1)S(1)} %get-tuple-element.14.hot_ref, f32[512,128]{1,0:T(8,128)S(1)} %get-tuple-element.15.edge_ref, ...), custom_call_target="tpu_custom_call" | custom-call | flops 4000000000 | bytes 20000000 | tf_op jit(solution)/shard_map/advance/pallas_call | solution.py:482
Async XLA Ops:
  0.0 3.1 %copy-start = (f32[14,8,64,256]{3,2,1,0:T(8,128)S(1)}, f32[14,8,64,256]{3,2,1,0:T(8,128)}, u32[]{:S(2)}) copy-start(f32[14,8,64,256]{3,2,1,0:T(8,128)} %u_ref.3) | copy-start | bytes 22020100
  3.1 7.5 %copy-start.1 = (f32[14,8,64,256]{3,2,1,0:T(8,128)S(1)}, f32[14,8,64,256]{3,2,1,0:T(8,128)}, u32[]{:S(2)}) copy-start(f32[14,8,64,256]{3,2,1,0:T(8,128)} %u_ref.3) | copy-start | bytes 22020100
  3.1 7.5 %copy-start.4 = (s32[1,1,1,128]{3,2,1,0:T(1,128)S(1)}, s32[1,1,1,128]{3,2,1,0:T(1,128)}, u32[]{:S(2)}) copy-start(s32[1,1,1,128]{3,2,1,0:T(1,128)} %row_ref.1) | copy-start | bytes 1540
  4.6 5.9 %collective-permute-start = (f32[512,128]{1,0:T(8,128)S(1)}, f32[512,128]{1,0:T(8,128)S(1)}, u32[]{:S(2)}, u32[]{:S(2)}) collective-permute-start(f32[512,128]{1,0:T(8,128)S(1)} %get-tuple-element.12), channel_id=1, source_target_pairs={{0,1},{1,0},{2,3},{3,2},{4,5},{5,4},{6,7},{7,6},{8,9},{9,8},{10,11... | collective-permute-start | bytes 786440 | tf_op jit(solution)/shard_map/ppermute | solution.py:100
  5.1 19.3 %collective-permute-start.1 = (f32[3,14,8,256]{3,2,1,0:T(8,128)S(1)}, f32[3,14,8,256]{3,2,1,0:T(8,128)S(1)}, u32[]{:S(2)}, u32[]{:S(2)}) collective-permute-start(f32[3,14,8,256]{3,2,1,0:T(8,128)S(1)} %get-tuple-element.17), channel_id=1, source_target_pairs={{0,2},{2,4},{4,6},{6,0},{1,3},{3,5},{5,7},{7,1},{8,10},{10,12},{12... | collective-permute-start | bytes 1032200 | tf_op jit(solution)/shard_map/ppermute | solution.py:505
  7.8 17.5 %collective-permute-start.2 = (f32[3,14,8,256]{3,2,1,0:T(8,128)S(1)}, f32[3,14,8,256]{3,2,1,0:T(8,128)S(1)}, u32[]{:S(2)}, u32[]{:S(2)}) collective-permute-start(f32[3,14,8,256]{3,2,1,0:T(8,128)S(1)} %get-tuple-element.18), channel_id=1, source_target_pairs={{2,0},{4,2},{6,4},{0,6},{3,1},{5,3},{7,5},{1,7},{10,8},{12,10},{14... | collective-permute-start | bytes 1032200 | tf_op jit(solution)/shard_map/ppermute | solution.py:506
  10.6 0.7 %copy-start.2 = (f32[14,14]{1,0:T(8,128)S(1)}, f32[14,14]{1,0:T(8,128)}, u32[]{:S(2)}) copy-start(f32[14,14]{1,0:T(8,128)} %left_ref.1) | copy-start | bytes 2356
  11.3 0.7 %copy-start.3 = (f32[14,14]{1,0:T(8,128)S(1)}, f32[14,14]{1,0:T(8,128)}, u32[]{:S(2)}) copy-start(f32[14,14]{1,0:T(8,128)} %right_ref.1) | copy-start | bytes 2356

commit v4 on v3

--- a/solution.py
+++ b/solution.py
@@ -52,16 +52,38 @@
     return result
 
 
-def pack_kernel(u_ref, tail_ref, head_ref, face_ref, row_sem):
-    _, cells_x, cells_y, cells_z = u_ref.shape
+def pack_y_kernel(u_ref, tail_ref, head_ref, first_ref, sem):
+    cells_x, cells_y = u_ref.shape[1], u_ref.shape[2]
     for x in range(cells_x):
         for j in range(WIDTH):
             pltpu.make_async_copy(
-                u_ref.at[:, x, pl.ds(cells_y - WIDTH + j, 1), :], tail_ref.at[j, :, pl.ds(x, 1), :], row_sem
+                u_ref.at[:, x, pl.ds(cells_y - WIDTH + j, 1), :], tail_ref.at[j, :, pl.ds(x, 1), :], sem
             ).start()
             pltpu.make_async_copy(
-                u_ref.at[:, x, pl.ds(j, 1), :], head_ref.at[j, :, pl.ds(x, 1), :], row_sem
+                u_ref.at[:, x, pl.ds(j, 1), :], head_ref.at[j, :, pl.ds(x, 1), :], sem
             ).start()
+    first_ref[...] = jnp.zeros_like(first_ref)
+    pltpu.make_async_copy(tail_ref, tail_ref, sem).wait()
+    pltpu.make_async_copy(head_ref, head_ref, sem).wait()
+
+
+def pack_y(conserved):
+    cells_x, cells_z = conserved.shape[1], conserved.shape[3]
+    face = jax.ShapeDtypeStruct((WIDTH, VARIABLES, cells_x, cells_z), F32)
+    return pl.pallas_call(
+        pack_y_kernel,
+        out_shape=[face, face, jax.ShapeDtypeStruct((8, LANES), F32)],
+        in_specs=[pl.BlockSpec(memory_space=pl.ANY)],
+        out_specs=[pl.BlockSpec(memory_space=pltpu.VMEM)] * 3,
+        scratch_shapes=[pltpu.SemaphoreType.DMA(())],
+        compiler_params=pltpu.CompilerParams(vmem_limit_bytes=16 << 20),
+        cost_estimate=pl.CostEstimate(flops=0, bytes_accessed=2_000_000, transcendentals=0),
+        name="pack_y",
+    )(conserved)
+
+
+def pack_z_kernel(u_ref, first_ref, basis_ref, wanted_ref, face_ref):
+    _, cells_x, cells_y, cells_z = u_ref.shape
     lane = lax.broadcasted_iota(jnp.int32, (cells_y, LANES), 1)
     for x in range(cells_x):
         packed = jnp.zeros((cells_y, LANES), F32)
@@ -69,27 +91,20 @@
             both = jnp.where(lane < LANES // 2, u_ref[v, x, :, :LANES], u_ref[v, x, :, cells_z - LANES :])
             packed = jnp.where(lane >> 3 == v, pltpu.roll(both, 8 * v + WIDTH, 1), packed)
         face_ref[x * cells_y : (x + 1) * cells_y, :] = packed
-    pltpu.make_async_copy(tail_ref, tail_ref, row_sem).wait()
-    pltpu.make_async_copy(head_ref, head_ref, row_sem).wait()
-
-
-def pack(conserved):
-    _, cells_x, cells_y, cells_z = conserved.shape
-    rows = jax.ShapeDtypeStruct((WIDTH, VARIABLES, cells_x, cells_z), F32)
+
+
+def pack_z(conserved, first, basis, wanted):
+    _, cells_x, cells_y, _ = conserved.shape
+    whole = pl.BlockSpec(memory_space=pltpu.VMEM)
     return pl.pallas_call(
-        pack_kernel,
-        out_shape=[
-            rows,
-            rows,
-            jax.ShapeDtypeStruct((cells_x * cells_y, LANES), F32),
-        ],
-        in_specs=[pl.BlockSpec(memory_space=pltpu.VMEM)],
-        out_specs=[pl.BlockSpec(memory_space=pltpu.VMEM)] * 3,
-        scratch_shapes=[pltpu.SemaphoreType.DMA(())],
+        pack_z_kernel,
+        out_shape=jax.ShapeDtypeStruct((cells_x * cells_y, LANES), F32),
+        in_specs=[whole] * 4,
+        out_specs=whole,
         compiler_params=pltpu.CompilerParams(vmem_limit_bytes=16 << 20),
         cost_estimate=pl.CostEstimate(flops=4_000_000, bytes_accessed=9_000_000, transcendentals=0),
-        name="pack",
-    )(conserved)
+        name="pack_z",
+    )(conserved, first, basis, wanted)
 
 
 def exchange_z(packed):
@@ -126,12 +141,10 @@
 
 def shock_kernel(
     list_ref,
-    count_ref,
+    wanted_ref,
     u_ref,
     face_ref,
-    left_ref,
-    right_ref,
-    row_ref,
+    basis_ref,
     change_ref,
     hot_ref,
     edge_ref,
@@ -151,20 +164,18 @@
     edge_t,
 ):
     _, cells_x, cells_y, cells_z = u_ref.shape
-    slots = row_ref.shape[-1]
+    slots = wanted_ref.shape[-1]
     total = cells_x * cells_y
     span = turned.shape[1]
 
     def fetch(p):
-        place = list_ref[0, 0, 0, p]
+        place = jnp.maximum(list_ref[0, p], 0)
         x, y = place // cells_y, place % cells_y
         for v in range(VARIABLES):
             pencils[v, pl.ds(p, 1), :] = u_ref[v, x, pl.ds(y, 1), :]
 
 
-    live = count_ref[0, 0, 0]
-    lane_slots = lax.broadcasted_iota(jnp.int32, (1, slots), 1)
-    wanted = jnp.where(lane_slots < live, row_ref[0, 0], -1)
+    wanted = wanted_ref[...]
     scale = time_step / 60.0
 
     for begin in range(0, total, LANES):
@@ -189,11 +200,11 @@
         hot_ref[wide, :slots] = hot
         hot_ref[wide, slots:] = hot
 
-    left_high, left_low = spread_matrix(0.5 * left_ref[...])
-    right_high, right_low = spread_matrix((time_step / 3.0) * right_ref[...])
+    left_high, left_low = spread_matrix(basis_ref[0])
+    right_high, right_low = spread_matrix(basis_ref[1])
 
     def neighbour(p, carry):
-        speed_t[pl.ds(p, 1), :] = face_ref[pl.ds(list_ref[0, 0, 0, p], 1), :]
+        speed_t[pl.ds(p, 1), :] = face_ref[pl.ds(jnp.maximum(list_ref[0, p], 0), 1), :]
         return carry
 
     lax.fori_loop(0, slots, neighbour, 0, unroll=8)
@@ -320,7 +331,7 @@
 
     lax.fori_loop(0, VARIABLES, upwind, 0)
 
-    keep = lane_slots < live
+    keep = wanted >= 0
 
     def back(index, carry):
         base = pl.multiple_of(index * 2 * GROUP, 2 * GROUP)
@@ -348,9 +359,9 @@
     lax.fori_loop(0, cells_z // (2 * GROUP), back, 0, unroll=True)
 
 
-def shock(listed, count, conserved, face, char_left, char_right):
+def shock(wanted, conserved, face, basis):
     _, cells_x, cells_y, cells_z = conserved.shape
-    slots = listed.shape[-1]
+    slots = wanted.shape[-1]
     total = cells_x * cells_y
     span = -(-(cells_z + 2 * LEAD) // GROUP) * GROUP
     vmem = pltpu.VMEM
@@ -380,13 +391,13 @@
             jax.ShapeDtypeStruct((total, LANES), F32),
             jax.ShapeDtypeStruct((4, total, cells_z), F32),
         ],
-        in_specs=[smem, smem, whole, whole, whole, whole, whole],
+        in_specs=[smem, whole, whole, whole, whole],
         out_specs=[whole] * 4,
         scratch_shapes=scratch,
         compiler_params=pltpu.CompilerParams(vmem_limit_bytes=24 << 20),
-        cost_estimate=pl.CostEstimate(flops=6_000_000_000, bytes_accessed=14_000_000, transcendentals=4_000_000),
+        cost_estimate=pl.CostEstimate(flops=100_000_000, bytes_accessed=1_000_000, transcendentals=0),
         name="shock",
-    )(listed, count, conserved, face, char_left, char_right, listed)
+    )(wanted, wanted, conserved, face, basis)
 
 
 def advance_kernel(
@@ -501,12 +512,15 @@
 def on_device(conserved, char_left, char_right, shock_list, shock_count):
     count = lax.axis_size("gy")
     ahead = [(i, (i + 1) % count) for i in range(count)]
-    tail, head, packed = pack(conserved)
+    tail, head, first = pack_y(conserved)
     before = lax.ppermute(tail, "gy", ahead)
     after = lax.ppermute(head, "gy", [(b, a) for a, b in ahead])
-    face = exchange_z(packed)
+    basis = jnp.stack([0.5 * char_left, (time_step / 3.0) * char_right])
+    slots = shock_list.shape[-1]
+    wanted = jnp.where(jnp.arange(slots, dtype=jnp.int32) < shock_count, shock_list, -1).reshape(1, slots)
+    face = exchange_z(pack_z(conserved, first, basis, wanted))
     change, hot, edge, state = shock(
-        shock_list, shock_count, conserved, face, char_left, char_right
+        wanted, conserved, face, basis
     )
     return advance(conserved, change, hot, edge, state, before, after)
 

time: 33.1 us -> 32.1 us (0.970)
  local copies, waits for them, and re-layouts: 4.48 us -> 3.11 us
  waiting for transfers between devices: 0.87 us -> 1.53 us
    ppermute x1, waiting for transfers between devices: 0.01 us -> 1.52 us  [exchange_z(): from_left = lax.ppermute(packed, 'gz', ahead)]
    unnamed x10 -> x12, local copies, waits for them, and re-layouts: 4.48 us -> 3.11 us
    ppermute x1, waiting for transfers between devices: 0.87 us -> 0.01 us  [on_device(): after = lax.ppermute(head, 'gy', [(b, a) for a, b in ahead])]
    ppermute x1, starting transfers between devices: 0.52 us -> 0.07 us  [exchange_z(): from_left = lax.ppermute(packed, 'gz', ahead)]
    ppermute x1, starting transfers between devices: 2.64 us -> 3.08 us  [on_device(): before = lax.ppermute(tail, 'gy', ahead)]
    pallas_call x1 -> x2, Pallas kernels: 1.53 us -> 1.53 us  [the longest x1 1.01 us: pack_z(): pl.pallas_call(pack_z_kernel, out_shape=jax.ShapeDtypeStruct((cells_x * c...]
  transfers between devices with their start and end apart: 3 -> 3, of which waited for: 1 -> 1; matrix products, arithmetic and copies ran while one was open for 0% -> 0% of each run, Pallas kernels for 38% -> 41%
where the time goes in v4:
time: 32.1 us; the launch traced here: 32 us
  Pallas kernels  21.2 us (66%)
  starting transfers between devices  5.24 us (16%)
  local copies, waits for them, and re-layouts  3.11 us (10%)
  waiting for transfers between devices  1.53 us (5%)
  between operations  0.92 us (3%)
    pallas_call x1, Pallas kernels, shock(): pl.pallas_call(shock_kernel, out_shape=[jax.ShapeDtypeStruct((VARIABLES,...  12.2 us
    pallas_call x1, Pallas kernels, advance(): pl.pallas_call(advance_kernel, out_shape=jax.ShapeDtypeStruct((VARIABLES,...  7.44 us
    unnamed x12, local copies, waits for them, and re-layouts  3.11 us
    ppermute x1, starting transfers between devices, on_device(): before = lax.ppermute(tail, 'gy', ahead)  3.08 us
    ppermute x1, starting transfers between devices, on_device(): after = lax.ppermute(head, 'gy', [(b, a) for a, b in ahead])  2.09 us
    ppermute x1, waiting for transfers between devices, exchange_z(): from_left = lax.ppermute(packed, 'gz', ahead)  1.52 us
    pallas_call x1, Pallas kernels, pack_z(): pl.pallas_call(pack_z_kernel, out_shape=jax.ShapeDtypeStruct((cells_x * c...  1.01 us
  transfers between devices with their start and end apart: 3, of which 1 were waited for; matrix products, arithmetic and copies ran while one was open for 0% of the time, Pallas kernels for 41%

profile of v4, /device:TPU:0, one launch (start us, length us, event | category | flops | bytes accessed | tf_op | source)
XLA Modules:
  0.0 32.0 jit_solution(17741535443296274149)
XLA Ops:
  0.0 0.0 copy-start
  0.0 3.1 %copy-done = f32[14,8,64,256]{3,2,1,0:T(8,128)S(1)} copy-done((f32[14,8,64,256]{3,2,1,0:T(8,128)S(1)}, f32[14,8,64,256]{3,2,1,0:T(8,128)}, u32[]{:S(2)}) %copy-start) | copy-done | bytes 7340056
  3.1 0.0 copy-start.3
  3.1 0.0 copy-start.1
  3.1 0.0 copy-start.2
  3.1 0.0 slice-start
  3.1 0.5 %pack_y.1 = (f32[3,14,8,256]{3,2,1,0:T(8,128)S(1)}, f32[3,14,8,256]{3,2,1,0:T(8,128)S(1)}, f32[8,128]{1,0:T(8,128)S(1)}) custom-call(f32[14,8,64,256]{3,2,1,0:T(8,128)S(1)} %copy-done), custom_call_target="tpu_custom_call" | custom-call | bytes 2000000 | tf_op jit(solution)/shard_map/pack_y/pallas_call | solution.py:73
  3.6 3.1 %collective-permute-start.1 = (f32[3,14,8,256]{3,2,1,0:T(8,128)S(1)}, f32[3,14,8,256]{3,2,1,0:T(8,128)S(1)}, u32[]{:S(2)}, u32[]{:S(2)}) collective-permute-start(f32[3,14,8,256]{3,2,1,0:T(8,128)S(1)} %get-tuple-element.17), channel_id=1, source_target_pairs={{0,2},{2,4},{4,6},{6,0},{1,3},{3,5},{5,7},{7,1},{8,10},{10,12},{12... | collective-permute-start | bytes 1032200 | tf_op jit(solution)/shard_map/ppermute | solution.py:516
  6.7 2.1 %collective-permute-start.2 = (f32[3,14,8,256]{3,2,1,0:T(8,128)S(1)}, f32[3,14,8,256]{3,2,1,0:T(8,128)S(1)}, u32[]{:S(2)}, u32[]{:S(2)}) collective-permute-start(f32[3,14,8,256]{3,2,1,0:T(8,128)S(1)} %get-tuple-element.18), channel_id=1, source_target_pairs={{2,0},{4,2},{6,4},{0,6},{3,1},{5,3},{7,5},{1,7},{10,8},{12,10},{14... | collective-permute-start | bytes 1032200 | tf_op jit(solution)/shard_map/ppermute | solution.py:517
  9.4 0.0 copy-done.3
  9.5 0.0 copy-done.1
  9.5 0.0 copy-done.2
  9.5 0.0 slice-start.1
  9.5 1.0 %pack_z.1 = f32[512,128]{1,0:T(8,128)S(1)} custom-call(f32[14,8,64,256]{3,2,1,0:T(8,128)S(1)} %copy-done, f32[8,128]{1,0:T(8,128)S(1)} %get-tuple-element.12.first_ref, f32[2,14,14]{2,1,0:T(8,128)S(1)} %pad_maximum_fusion.basis_ref, s32[1,128]{1,0:T(1,128)S(1)} %fusion.wanted_ref.list_ref), custom_call_target="tpu_custom_call" | custom-call | flops 4000000 | bytes 9000000 | tf_op jit(solution)/shard_map/pack_z/pallas_call | solution.py:99
  10.5 0.1 collective-permute-start
  10.6 1.5 %collective-permute-done.face_ref = f32[512,128]{1,0:T(8,128)S(1)} collective-permute-done((f32[512,128]{1,0:T(8,128)S(1)}, f32[512,128]{1,0:T(8,128)S(1)}, u32[]{:S(2)}, u32[]{:S(2)}) %collective-permute-start) | collective-permute-done | bytes 262176 | tf_op jit(solution)/shard_map/ppermute | solution.py:115
  12.1 0.0 slice-done
  12.1 0.0 slice-done.1
  12.1 12.2 %shock.1 = (bf16[14,256,256]{2,1,0:T(8,128)(2,1)S(1)}, bf16[512,256]{1,0:T(8,128)(2,1)S(1)}, f32[512,128]{1,0:T(8,128)S(1)}, f32[4,512,256]{2,1,0:T(8,128)S(1)}) custom-call(s32[1,128]{1,0:T(1,128)S(1)} %fusion.wanted_ref.list_ref, s32[1,128]{1,0:T(1,128)S(1)} %fusion.wanted_ref.list_ref, f32[14,8,64,256]{3,2,1,0:T(8,128)S(1)} %bitcast.11, ...), custom_call_target="tpu_custom_call" | custom-call | flops 100000000 | bytes 1000000 | tf_op jit(solution)/shard_map/shock/pallas_call | solution.py:386
  24.3 0.0 collective-permute-done.1.before_ref
  24.4 0.0 collective-permute-done.2.after_ref
  24.4 7.4 %advance.1 = f32[14,512,256]{2,1,0:T(8,128)} custom-call(f32[14,512,256]{2,1,0:T(8,128)S(1)} %bitcast.12, bf16[14,256,256]{2,1,0:T(8,128)(2,1)S(1)} %get-tuple-element.13.change_ref, bf16[512,256]{1,0:T(8,128)(2,1)S(1)} %get-tuple-element.14.hot_ref, f32[512,128]{1,0:T(8,128)S(1)} %get-tuple-element.15.edge_ref, ...), custom_call_target="tpu_custom_call" | custom-call | flops 4000000000 | bytes 20000000 | tf_op jit(solution)/shard_map/advance/pallas_call | solution.py:493
  (4 shorter events, 0.0 us)
Async XLA Ops:
  0.0 3.1 %copy-start = (f32[14,8,64,256]{3,2,1,0:T(8,128)S(1)}, f32[14,8,64,256]{3,2,1,0:T(8,128)}, u32[]{:S(2)}) copy-start(f32[14,8,64,256]{3,2,1,0:T(8,128)} %u_ref.5) | copy-start | bytes 22020100
  3.1 6.4 %copy-start.3 = (s32[1,1,1,128]{3,2,1,0:T(1,128)S(1)}, s32[1,1,1,128]{3,2,1,0:T(1,128)}, u32[]{:S(2)}) copy-start(s32[1,1,1,128]{3,2,1,0:T(1,128)} %param.8) | copy-start | bytes 1540
  3.1 6.4 %copy-start.1 = (f32[14,14]{1,0:T(8,128)S(1)}, f32[14,14]{1,0:T(8,128)}, u32[]{:S(2)}) copy-start(f32[14,14]{1,0:T(8,128)} %param.7) | copy-start | bytes 2356
  3.1 6.4 %copy-start.2 = (f32[14,14]{1,0:T(8,128)S(1)}, f32[14,14]{1,0:T(8,128)}, u32[]{:S(2)}) copy-start(f32[14,14]{1,0:T(8,128)} %param.6) | copy-start | bytes 2356
  3.1 9.1 %slice-start = ((s8[7340032]{0:T(1024)(128)(4,1)}), s8[4194304]{0:T(1024)(128)(4,1)S(1)}, s32[]{:S(2)}) async-start(s8[7340032]{0:T(1024)(128)(4,1)} %bitcast.10), calls=%async_computation | async-start | bytes 8388608
  3.6 20.7 %collective-permute-start.1 = (f32[3,14,8,256]{3,2,1,0:T(8,128)S(1)}, f32[3,14,8,256]{3,2,1,0:T(8,128)S(1)}, u32[]{:S(2)}, u32[]{:S(2)}) collective-permute-start(f32[3,14,8,256]{3,2,1,0:T(8,128)S(1)} %get-tuple-element.17), channel_id=1, source_target_pairs={{0,2},{2,4},{4,6},{6,0},{1,3},{3,5},{5,7},{7,1},{8,10},{10,12},{12... | collective-permute-start | bytes 1032200 | tf_op jit(solution)/shard_map/ppermute | solution.py:516
  6.7 17.7 %collective-permute-start.2 = (f32[3,14,8,256]{3,2,1,0:T(8,128)S(1)}, f32[3,14,8,256]{3,2,1,0:T(8,128)S(1)}, u32[]{:S(2)}, u32[]{:S(2)}) collective-permute-start(f32[3,14,8,256]{3,2,1,0:T(8,128)S(1)} %get-tuple-element.18), channel_id=1, source_target_pairs={{2,0},{4,2},{6,4},{0,6},{3,1},{5,3},{7,5},{1,7},{10,8},{12,10},{14... | collective-permute-start | bytes 1032200 | tf_op jit(solution)/shard_map/ppermute | solution.py:517
  9.5 2.6 %slice-start.1 = ((s8[7340032]{0:T(1024)(128)(4,1)}), s8[3145728]{0:T(1024)(128)(4,1)S(1)}, s32[]{:S(2)}) async-start(s8[7340032]{0:T(1024)(128)(4,1)} %bitcast.10), calls=%async_computation.1 | async-start | bytes 6291456
  10.5 1.6 %collective-permute-start = (f32[512,128]{1,0:T(8,128)S(1)}, f32[512,128]{1,0:T(8,128)S(1)}, u32[]{:S(2)}, u32[]{:S(2)}) collective-permute-start(f32[512,128]{1,0:T(8,128)S(1)} %pack_z.1), channel_id=1, source_target_pairs={{0,1},{1,0},{2,3},{3,2},{4,5},{5,4},{6,7},{7,6},{8,9},{9,8},{10,11... | collective-permute-start | bytes 786440 | tf_op jit(solution)/shard_map/ppermute | solution.py:115

commit v5 on v4

--- a/solution.py
+++ b/solution.py
@@ -139,17 +139,67 @@
     return jnp.where(offset < 0, -weight, weight)
 
 
+def prepare_kernel(list_ref, wanted_ref, u_ref, face_ref, state_ref, pencils):
+    _, cells_x, cells_y, cells_z = u_ref.shape
+    slots = wanted_ref.shape[-1]
+    total = cells_x * cells_y
+    scale = time_step / 60.0
+    wanted = wanted_ref[...]
+
+    def fetch(p):
+        place = jnp.maximum(list_ref[0, p], 0)
+        x, y = place // cells_y, place % cells_y
+        for v in range(VARIABLES):
+            pencils[v, pl.ds(p, 1), :] = u_ref[v, x, pl.ds(y, 1), :]
+
+    def state(index, carry):
+        at = slice(index * 8, index * 8 + 8)
+        x, y = index * 8 // cells_y, index * 8 % cells_y
+        pencil = index * 8 + lax.broadcasted_iota(jnp.int32, (8, slots), 0)
+        calm = scale - scale * jnp.sum((wanted == pencil).astype(F32), axis=1, keepdims=True)
+        for begin in range(0, cells_z, LANES):
+            wide = slice(begin, begin + LANES)
+            parts = [u_ref[v, x, y : y + 8, wide] for v in range(VARIABLES)]
+            inverse, pressure = state_of(parts)
+            state_ref[0, at, wide] = parts[SPECIES + 1] * (inverse * scale)
+            state_ref[1, at, wide] = parts[SPECIES + 2] * (inverse * calm)
+            state_ref[2, at, wide] = pressure
+            state_ref[3, at, wide] = pressure * calm
+        return carry
+
+    for index in range(total // 8):
+        state(index, 0)
+        for p in range(index * 8 * slots // total, (index + 1) * 8 * slots // total):
+            fetch(p)
+
+
+def prepare(wanted, conserved, packed):
+    _, cells_x, cells_y, cells_z = conserved.shape
+    slots = wanted.shape[-1]
+    whole = pl.BlockSpec(memory_space=pltpu.VMEM)
+    return pl.pallas_call(
+        prepare_kernel,
+        out_shape=[
+            jax.ShapeDtypeStruct((4, cells_x * cells_y, cells_z), F32),
+            jax.ShapeDtypeStruct((VARIABLES, slots, cells_z), F32),
+        ],
+        in_specs=[pl.BlockSpec(memory_space=pltpu.SMEM), whole, whole, whole],
+        out_specs=[whole] * 2,
+        compiler_params=pltpu.CompilerParams(vmem_limit_bytes=16 << 20),
+        cost_estimate=pl.CostEstimate(flops=8_000_000, bytes_accessed=9_000_000, transcendentals=0),
+        name="prepare",
+    )(wanted, wanted, conserved, packed)
+
+
 def shock_kernel(
     list_ref,
     wanted_ref,
-    u_ref,
+    pencils,
     face_ref,
     basis_ref,
     change_ref,
     hot_ref,
     edge_ref,
-    state_ref,
-    pencils,
     turned,
     speed_t,
     press_t,
@@ -163,16 +213,10 @@
     faces,
     edge_t,
 ):
-    _, cells_x, cells_y, cells_z = u_ref.shape
     slots = wanted_ref.shape[-1]
-    total = cells_x * cells_y
+    total = face_ref.shape[0]
+    cells_z = pencils.shape[2]
     span = turned.shape[1]
-
-    def fetch(p):
-        place = jnp.maximum(list_ref[0, p], 0)
-        x, y = place // cells_y, place % cells_y
-        for v in range(VARIABLES):
-            pencils[v, pl.ds(p, 1), :] = u_ref[v, x, pl.ds(y, 1), :]
 
 
     wanted = wanted_ref[...]
@@ -209,26 +253,6 @@
 
     lax.fori_loop(0, slots, neighbour, 0, unroll=8)
     border = speed_t[0:slots, :].T
-
-    def state(index, carry):
-        at = slice(index * 8, index * 8 + 8)
-        x, y = index * 8 // cells_y, index * 8 % cells_y
-        pencil = index * 8 + lax.broadcasted_iota(jnp.int32, (8, slots), 0)
-        calm = scale - scale * jnp.sum((wanted == pencil).astype(F32), axis=1, keepdims=True)
-        for begin in range(0, cells_z, LANES):
-            wide = slice(begin, begin + LANES)
-            parts = [u_ref[v, x, y : y + 8, wide] for v in range(VARIABLES)]
-            inverse, pressure = state_of(parts)
-            state_ref[0, at, wide] = parts[SPECIES + 1] * (inverse * scale)
-            state_ref[1, at, wide] = parts[SPECIES + 2] * (inverse * calm)
-            state_ref[2, at, wide] = pressure
-            state_ref[3, at, wide] = pressure * calm
-        return carry
-
-    for index in range(total // 8):
-        state(index, 0)
-        for p in range(index * 8 * slots // total, (index + 1) * 8 * slots // total):
-            fetch(p)
 
     for v in range(VARIABLES):
         tile = border[8 * v : 8 * v + 8, :]
@@ -359,15 +383,14 @@
     lax.fori_loop(0, cells_z // (2 * GROUP), back, 0, unroll=True)
 
 
-def shock(wanted, conserved, face, basis):
-    _, cells_x, cells_y, cells_z = conserved.shape
+def shock(wanted, pencils, face, basis):
+    cells_z = pencils.shape[2]
     slots = wanted.shape[-1]
-    total = cells_x * cells_y
+    total = face.shape[0]
     span = -(-(cells_z + 2 * LEAD) // GROUP) * GROUP
     vmem = pltpu.VMEM
     work = vmem((2, span + 8, slots), F32)
     scratch = [
-        vmem((VARIABLES, slots, cells_z), F32),
         vmem((VARIABLES, span, slots), F32),
         vmem((span, slots), F32),
         vmem((span, slots), F32),
@@ -389,15 +412,14 @@
             jax.ShapeDtypeStruct((VARIABLES, cells_z, 2 * slots), BF16),
             jax.ShapeDtypeStruct((total, 2 * slots), BF16),
             jax.ShapeDtypeStruct((total, LANES), F32),
-            jax.ShapeDtypeStruct((4, total, cells_z), F32),
         ],
         in_specs=[smem, whole, whole, whole, whole],
-        out_specs=[whole] * 4,
+        out_specs=[whole] * 3,
         scratch_shapes=scratch,
         compiler_params=pltpu.CompilerParams(vmem_limit_bytes=24 << 20),
         cost_estimate=pl.CostEstimate(flops=100_000_000, bytes_accessed=1_000_000, transcendentals=0),
         name="shock",
-    )(wanted, wanted, conserved, face, basis)
+    )(wanted, wanted, pencils, face, basis)
 
 
 def advance_kernel(
@@ -518,10 +540,10 @@
     basis = jnp.stack([0.5 * char_left, (time_step / 3.0) * char_right])
     slots = shock_list.shape[-1]
     wanted = jnp.where(jnp.arange(slots, dtype=jnp.int32) < shock_count, shock_list, -1).reshape(1, slots)
-    face = exchange_z(pack_z(conserved, first, basis, wanted))
-    change, hot, edge, state = shock(
-        wanted, conserved, face, basis
-    )
+    packed = pack_z(conserved, first, basis, wanted)
+    face = exchange_z(packed)
+    state, pencils = prepare(wanted, conserved, packed)
+    change, hot, edge = shock(wanted, pencils, face, basis)
     return advance(conserved, change, hot, edge, state, before, after)
 
 

time: 32.1 us -> 32.1 us (level)
  waiting for transfers between devices: 1.53 us -> 0.3 us
  Pallas kernels: 21.2 us -> 22.3 us
    pallas_call x0 -> x1, Pallas kernels: none -> 2.12 us  [prepare(): pl.pallas_call(prepare_kernel, out_shape=[jax.ShapeDtypeStruct((4, cells_...]
    pallas_call x1, Pallas kernels: 12.2 us -> 10.5 us  [shock(): pl.pallas_call(shock_kernel, out_shape=[jax.ShapeDtypeStruct((VARIABLES,...]
    ppermute x1, waiting for transfers between devices: 1.52 us -> 0.01 us  [exchange_z(): from_left = lax.ppermute(packed, 'gz', ahead)]
    pallas_call x1, Pallas kernels: 7.44 us -> 8.17 us  [advance(): pl.pallas_call(advance_kernel, out_shape=jax.ShapeDtypeStruct((VARIABLES,...]
  transfers between devices with their start and end apart: 3 -> 3, of which waited for: 1 -> 1; matrix products, arithmetic and copies ran while one was open for 0% -> 0% of each run, Pallas kernels for 41% -> 43%
where the time goes in v5:
time: 32.1 us; the launch traced here: 31.9 us
  Pallas kernels  22.3 us (69%)
  starting transfers between devices  5.24 us (16%)
  local copies, waits for them, and re-layouts  3.11 us (10%)
  between operations  0.93 us (3%)
    pallas_call x1, Pallas kernels, shock(): pl.pallas_call(shock_kernel, out_shape=[jax.ShapeDtypeStruct((VARIABLES,...  10.5 us
    pallas_call x1, Pallas kernels, advance(): pl.pallas_call(advance_kernel, out_shape=jax.ShapeDtypeStruct((VARIABLES,...  8.17 us
    unnamed x12, local copies, waits for them, and re-layouts  3.11 us
    ppermute x1, starting transfers between devices, on_device(): before = lax.ppermute(tail, 'gy', ahead)  3.08 us
    pallas_call x1, Pallas kernels, prepare(): pl.pallas_call(prepare_kernel, out_shape=[jax.ShapeDtypeStruct((4, cells_...  2.12 us
    ppermute x1, starting transfers between devices, on_device(): after = lax.ppermute(head, 'gy', [(b, a) for a, b in ahead])  2.09 us
    pallas_call x1, Pallas kernels, pack_z(): pl.pallas_call(pack_z_kernel, out_shape=jax.ShapeDtypeStruct((cells_x * c...  1.01 us
  transfers between devices with their start and end apart: 3, of which 1 were waited for; matrix products, arithmetic and copies ran while one was open for 0% of the time, Pallas kernels for 43%

profile of v5, /device:TPU:0, one launch (start us, length us, event | category | flops | bytes accessed | tf_op | source)
XLA Modules:
  0.0 31.9 jit_solution(123407153519798236)
XLA Ops:
  0.0 0.0 copy-start
  0.0 3.1 %copy-done = f32[14,8,64,256]{3,2,1,0:T(8,128)S(1)} copy-done((f32[14,8,64,256]{3,2,1,0:T(8,128)S(1)}, f32[14,8,64,256]{3,2,1,0:T(8,128)}, u32[]{:S(2)}) %copy-start) | copy-done | bytes 7340056
  3.1 0.0 copy-start.3
  3.1 0.0 copy-start.1
  3.1 0.0 copy-start.2
  3.1 0.5 %pack_y.1 = (f32[3,14,8,256]{3,2,1,0:T(8,128)S(1)}, f32[3,14,8,256]{3,2,1,0:T(8,128)S(1)}, f32[8,128]{1,0:T(8,128)S(1)}) custom-call(f32[14,8,64,256]{3,2,1,0:T(8,128)S(1)} %copy-done), custom_call_target="tpu_custom_call" | custom-call | bytes 2000000 | tf_op jit(solution)/shard_map/pack_y/pallas_call | solution.py:73
  3.6 3.1 %collective-permute-start.1 = (f32[3,14,8,256]{3,2,1,0:T(8,128)S(1)}, f32[3,14,8,256]{3,2,1,0:T(8,128)S(1)}, u32[]{:S(2)}, u32[]{:S(2)}) collective-permute-start(f32[3,14,8,256]{3,2,1,0:T(8,128)S(1)} %get-tuple-element.19), channel_id=1, source_target_pairs={{0,2},{2,4},{4,6},{6,0},{1,3},{3,5},{5,7},{7,1},{8,10},{10,12},{12... | collective-permute-start | bytes 1032200 | tf_op jit(solution)/shard_map/ppermute | solution.py:538
  6.7 2.1 %collective-permute-start.2 = (f32[3,14,8,256]{3,2,1,0:T(8,128)S(1)}, f32[3,14,8,256]{3,2,1,0:T(8,128)S(1)}, u32[]{:S(2)}, u32[]{:S(2)}) collective-permute-start(f32[3,14,8,256]{3,2,1,0:T(8,128)S(1)} %get-tuple-element.20), channel_id=1, source_target_pairs={{2,0},{4,2},{6,4},{0,6},{3,1},{5,3},{7,5},{1,7},{10,8},{12,10},{14... | collective-permute-start | bytes 1032200 | tf_op jit(solution)/shard_map/ppermute | solution.py:539
  9.4 0.0 copy-done.3
  9.5 0.0 copy-done.1
  9.5 0.0 copy-done.2
  9.5 0.0 slice-start
  9.5 1.0 %pack_z.1.face_ref = f32[512,128]{1,0:T(8,128)S(1)} custom-call(f32[14,8,64,256]{3,2,1,0:T(8,128)S(1)} %copy-done, f32[8,128]{1,0:T(8,128)S(1)} %get-tuple-element.13.first_ref, f32[2,14,14]{2,1,0:T(8,128)S(1)} %pad_maximum_fusion.basis_ref, s32[1,128]{1,0:T(1,128)S(1)} %fusion.wanted_ref.list_ref), custom_call_target="tpu_custom_call" | custom-call | flops 4000000 | bytes 9000000 | tf_op jit(solution)/shard_map/pack_z/pallas_call | solution.py:99
  10.5 0.0 slice-start.1
  10.5 0.1 collective-permute-start
  10.6 2.1 %prepare.1 = (f32[4,512,256]{2,1,0:T(8,128)S(1)}, f32[14,128,256]{2,1,0:T(8,128)S(1)}) custom-call(s32[1,128]{1,0:T(1,128)S(1)} %fusion.wanted_ref.list_ref, s32[1,128]{1,0:T(1,128)S(1)} %fusion.wanted_ref.list_ref, f32[14,8,64,256]{3,2,1,0:T(8,128)S(1)} %copy-done, f32[512,128]{1,0:T(8,128)S(1)} %pack_z.1.face_ref), custom_call_target="tpu_custom_call" | custom-call | flops 8000000 | bytes 9000000 | tf_op jit(solution)/shard_map/prepare/pallas_call | solution.py:180
  12.8 0.0 collective-permute-done.face_ref
  12.8 10.5 %shock.1 = (bf16[14,256,256]{2,1,0:T(8,128)(2,1)S(1)}, bf16[512,256]{1,0:T(8,128)(2,1)S(1)}, f32[512,128]{1,0:T(8,128)S(1)}) custom-call(s32[1,128]{1,0:T(1,128)S(1)} %fusion.wanted_ref.list_ref, s32[1,128]{1,0:T(1,128)S(1)} %fusion.wanted_ref.list_ref, f32[14,128,256]{2,1,0:T(8,128)S(1)} %get-tuple-element.14.pencils, ...), custom_call_target="tpu_custom_call" | custom-call | flops 100000000 | bytes 1000000 | tf_op jit(solution)/shard_map/shock/pallas_call | solution.py:409
  23.3 0.0 collective-permute-done.1.before_ref
  23.3 0.3 collective-permute-done.2.after_ref
  23.6 0.0 slice-done
  23.6 0.0 slice-done.1
  23.6 8.2 %advance.1 = f32[14,512,256]{2,1,0:T(8,128)} custom-call(f32[14,512,256]{2,1,0:T(8,128)S(1)} %bitcast.12, bf16[14,256,256]{2,1,0:T(8,128)(2,1)S(1)} %get-tuple-element.15.change_ref, bf16[512,256]{1,0:T(8,128)(2,1)S(1)} %get-tuple-element.16.hot_ref, f32[512,128]{1,0:T(8,128)S(1)} %get-tuple-element.17.edge_ref, ...), custom_call_target="tpu_custom_call" | custom-call | flops 4000000000 | bytes 20000000 | tf_op jit(solution)/shard_map/advance/pallas_call | solution.py:515
  (4 shorter events, 0.0 us)
Async XLA Ops:
  0.0 3.1 %copy-start = (f32[14,8,64,256]{3,2,1,0:T(8,128)S(1)}, f32[14,8,64,256]{3,2,1,0:T(8,128)}, u32[]{:S(2)}) copy-start(f32[14,8,64,256]{3,2,1,0:T(8,128)} %u_ref.5) | copy-start | bytes 22020100
  3.1 6.4 %copy-start.3 = (s32[1,1,1,128]{3,2,1,0:T(1,128)S(1)}, s32[1,1,1,128]{3,2,1,0:T(1,128)}, u32[]{:S(2)}) copy-start(s32[1,1,1,128]{3,2,1,0:T(1,128)} %param.8) | copy-start | bytes 1540
  3.1 6.4 %copy-start.1 = (f32[14,14]{1,0:T(8,128)S(1)}, f32[14,14]{1,0:T(8,128)}, u32[]{:S(2)}) copy-start(f32[14,14]{1,0:T(8,128)} %param.7) | copy-start | bytes 2356
  3.1 6.4 %copy-start.2 = (f32[14,14]{1,0:T(8,128)S(1)}, f32[14,14]{1,0:T(8,128)}, u32[]{:S(2)}) copy-start(f32[14,14]{1,0:T(8,128)} %param.6) | copy-start | bytes 2356
  3.6 19.7 %collective-permute-start.1 = (f32[3,14,8,256]{3,2,1,0:T(8,128)S(1)}, f32[3,14,8,256]{3,2,1,0:T(8,128)S(1)}, u32[]{:S(2)}, u32[]{:S(2)}) collective-permute-start(f32[3,14,8,256]{3,2,1,0:T(8,128)S(1)} %get-tuple-element.19), channel_id=1, source_target_pairs={{0,2},{2,4},{4,6},{6,0},{1,3},{3,5},{5,7},{7,1},{8,10},{10,12},{12... | collective-permute-start | bytes 1032200 | tf_op jit(solution)/shard_map/ppermute | solution.py:538
  6.7 16.9 %collective-permute-start.2 = (f32[3,14,8,256]{3,2,1,0:T(8,128)S(1)}, f32[3,14,8,256]{3,2,1,0:T(8,128)S(1)}, u32[]{:S(2)}, u32[]{:S(2)}) collective-permute-start(f32[3,14,8,256]{3,2,1,0:T(8,128)S(1)} %get-tuple-element.20), channel_id=1, source_target_pairs={{2,0},{4,2},{6,4},{0,6},{3,1},{5,3},{7,5},{1,7},{10,8},{12,10},{14... | collective-permute-start | bytes 1032200 | tf_op jit(solution)/shard_map/ppermute | solution.py:539
  9.5 14.1 %slice-start = ((s8[7340032]{0:T(1024)(128)(4,1)}), s8[4194304]{0:T(1024)(128)(4,1)S(1)}, s32[]{:S(2)}) async-start(s8[7340032]{0:T(1024)(128)(4,1)} %bitcast.10), calls=%async_computation | async-start | bytes 8388608
  10.5 13.1 %slice-start.1 = ((s8[7340032]{0:T(1024)(128)(4,1)}), s8[3145728]{0:T(1024)(128)(4,1)S(1)}, s32[]{:S(2)}) async-start(s8[7340032]{0:T(1024)(128)(4,1)} %bitcast.10), calls=%async_computation.1 | async-start | bytes 6291456
  10.5 2.2 %collective-permute-start = (f32[512,128]{1,0:T(8,128)S(1)}, f32[512,128]{1,0:T(8,128)S(1)}, u32[]{:S(2)}, u32[]{:S(2)}) collective-permute-start(f32[512,128]{1,0:T(8,128)S(1)} %pack_z.1.face_ref), channel_id=1, source_target_pairs={{0,1},{1,0},{2,3},{3,2},{4,5},{5,4},{6,7},{7,6},{8,9},{9,8},{10,11... | collective-permute-start | bytes 786440 | tf_op jit(solution)/shard_map/ppermute | solution.py:115

commit v6 on v4

--- a/solution.py
+++ b/solution.py
@@ -417,7 +417,7 @@
     column = lax.broadcasted_iota(jnp.int32, (rows, rows), 1)
     inside = row // cells_y == column // cells_y
     along_y = jnp.where(inside, stencil(column - row), 0.0).astype(BF16)
-    for turn in range(2):
+    for turn in range(1):
         for block in range(total // rows):
             for k in range(2):
                 left[turn, block, :, 2 * cells_z + k * rows : 2 * cells_z + k * rows + rows] = along_y
@@ -437,7 +437,7 @@
 
     lane = lax.broadcasted_iota(jnp.int32, (GROUP, LANES), 1)
     for v in range(VARIABLES):
-        turn = v % 2
+        turn = 0
 
         for begin in range(0, total, GROUP):
             at = slice(begin, begin + GROUP)
@@ -497,8 +497,8 @@
         out_specs=pl.BlockSpec(memory_space=pl.ANY),
         scratch_shapes=[
             pltpu.VMEM((VARIABLES, total, cells_z), F32),
-            pltpu.VMEM((2, total // rows, rows, 2 * (cells_z + rows)), BF16),
-            pltpu.VMEM((2, total // rows, 2 * (cells_z + rows), cells_z), BF16),
+            pltpu.VMEM((1, total // rows, rows, 2 * (cells_z + rows)), BF16),
+            pltpu.VMEM((1, total // rows, 2 * (cells_z + rows), cells_z), BF16),
             pltpu.VMEM((VARIABLES, cells_z // LANES, cells_x * 2 * GROUP, LANES), F32),
             pltpu.SemaphoreType.DMA(()),
         ],

time: 32.1 us -> 32.1 us (level)
  no operation moved by 1% of the time
where the time goes in v6:
time: 32.1 us; the launch traced here: 32 us
  Pallas kernels  21.2 us (66%)
  starting transfers between devices  5.24 us (16%)
  local copies, waits for them, and re-layouts  3.11 us (10%)
  waiting for transfers between devices  1.53 us (5%)
  between operations  0.92 us (3%)
    pallas_call x1, Pallas kernels, shock(): pl.pallas_call(shock_kernel, out_shape=[jax.ShapeDtypeStruct((VARIABLES,...  12.2 us
    pallas_call x1, Pallas kernels, advance(): pl.pallas_call(advance_kernel, out_shape=jax.ShapeDtypeStruct((VARIABLES,...  7.44 us
    unnamed x12, local copies, waits for them, and re-layouts  3.11 us
    ppermute x1, starting transfers between devices, on_device(): before = lax.ppermute(tail, 'gy', ahead)  3.08 us
    ppermute x1, starting transfers between devices, on_device(): after = lax.ppermute(head, 'gy', [(b, a) for a, b in ahead])  2.09 us
    ppermute x1, waiting for transfers between devices, exchange_z(): from_left = lax.ppermute(packed, 'gz', ahead)  1.52 us
    pallas_call x1, Pallas kernels, pack_z(): pl.pallas_call(pack_z_kernel, out_shape=jax.ShapeDtypeStruct((cells_x * c...  1.01 us
  transfers between devices with their start and end apart: 3, of which 1 were waited for; matrix products, arithmetic and copies ran while one was open for 0% of the time, Pallas kernels for 41%

profile of v6, /device:TPU:0, one launch (start us, length us, event | category | flops | bytes accessed | tf_op | source)
XLA Modules:
  0.0 32.0 jit_solution(17741535443296274149)
XLA Ops:
  0.0 0.0 copy-start
  0.0 3.1 %copy-done = f32[14,8,64,256]{3,2,1,0:T(8,128)S(1)} copy-done((f32[14,8,64,256]{3,2,1,0:T(8,128)S(1)}, f32[14,8,64,256]{3,2,1,0:T(8,128)}, u32[]{:S(2)}) %copy-start) | copy-done | bytes 7340056
  3.1 0.0 copy-start.3
  3.1 0.0 copy-start.1
  3.1 0.0 copy-start.2
  3.1 0.0 slice-start
  3.1 0.5 %pack_y.1 = (f32[3,14,8,256]{3,2,1,0:T(8,128)S(1)}, f32[3,14,8,256]{3,2,1,0:T(8,128)S(1)}, f32[8,128]{1,0:T(8,128)S(1)}) custom-call(f32[14,8,64,256]{3,2,1,0:T(8,128)S(1)} %copy-done), custom_call_target="tpu_custom_call" | custom-call | bytes 2000000 | tf_op jit(solution)/shard_map/pack_y/pallas_call | solution.py:73
  3.6 3.1 %collective-permute-start.1 = (f32[3,14,8,256]{3,2,1,0:T(8,128)S(1)}, f32[3,14,8,256]{3,2,1,0:T(8,128)S(1)}, u32[]{:S(2)}, u32[]{:S(2)}) collective-permute-start(f32[3,14,8,256]{3,2,1,0:T(8,128)S(1)} %get-tuple-element.17), channel_id=1, source_target_pairs={{0,2},{2,4},{4,6},{6,0},{1,3},{3,5},{5,7},{7,1},{8,10},{10,12},{12... | collective-permute-start | bytes 1032200 | tf_op jit(solution)/shard_map/ppermute | solution.py:516
  6.7 2.1 %collective-permute-start.2 = (f32[3,14,8,256]{3,2,1,0:T(8,128)S(1)}, f32[3,14,8,256]{3,2,1,0:T(8,128)S(1)}, u32[]{:S(2)}, u32[]{:S(2)}) collective-permute-start(f32[3,14,8,256]{3,2,1,0:T(8,128)S(1)} %get-tuple-element.18), channel_id=1, source_target_pairs={{2,0},{4,2},{6,4},{0,6},{3,1},{5,3},{7,5},{1,7},{10,8},{12,10},{14... | collective-permute-start | bytes 1032200 | tf_op jit(solution)/shard_map/ppermute | solution.py:517
  9.4 0.0 copy-done.3
  9.5 0.0 copy-done.1
  9.5 0.0 copy-done.2
  9.5 0.0 slice-start.1
  9.5 1.0 %pack_z.1 = f32[512,128]{1,0:T(8,128)S(1)} custom-call(f32[14,8,64,256]{3,2,1,0:T(8,128)S(1)} %copy-done, f32[8,128]{1,0:T(8,128)S(1)} %get-tuple-element.12.first_ref, f32[2,14,14]{2,1,0:T(8,128)S(1)} %pad_maximum_fusion.basis_ref, s32[1,128]{1,0:T(1,128)S(1)} %fusion.wanted_ref.list_ref), custom_call_target="tpu_custom_call" | custom-call | flops 4000000 | bytes 9000000 | tf_op jit(solution)/shard_map/pack_z/pallas_call | solution.py:99
  10.5 0.1 collective-permute-start
  10.6 1.5 %collective-permute-done.face_ref = f32[512,128]{1,0:T(8,128)S(1)} collective-permute-done((f32[512,128]{1,0:T(8,128)S(1)}, f32[512,128]{1,0:T(8,128)S(1)}, u32[]{:S(2)}, u32[]{:S(2)}) %collective-permute-start) | collective-permute-done | bytes 262176 | tf_op jit(solution)/shard_map/ppermute | solution.py:115
  12.1 0.0 slice-done
  12.1 0.0 slice-done.1
  12.1 12.2 %shock.1 = (bf16[14,256,256]{2,1,0:T(8,128)(2,1)S(1)}, bf16[512,256]{1,0:T(8,128)(2,1)S(1)}, f32[512,128]{1,0:T(8,128)S(1)}, f32[4,512,256]{2,1,0:T(8,128)S(1)}) custom-call(s32[1,128]{1,0:T(1,128)S(1)} %fusion.wanted_ref.list_ref, s32[1,128]{1,0:T(1,128)S(1)} %fusion.wanted_ref.list_ref, f32[14,8,64,256]{3,2,1,0:T(8,128)S(1)} %bitcast.11, ...), custom_call_target="tpu_custom_call" | custom-call | flops 100000000 | bytes 1000000 | tf_op jit(solution)/shard_map/shock/pallas_call | solution.py:386
  24.3 0.0 collective-permute-done.1.before_ref
  24.4 0.0 collective-permute-done.2.after_ref
  24.4 7.4 %advance.1 = f32[14,512,256]{2,1,0:T(8,128)} custom-call(f32[14,512,256]{2,1,0:T(8,128)S(1)} %bitcast.12, bf16[14,256,256]{2,1,0:T(8,128)(2,1)S(1)} %get-tuple-element.13.change_ref, bf16[512,256]{1,0:T(8,128)(2,1)S(1)} %get-tuple-element.14.hot_ref, f32[512,128]{1,0:T(8,128)S(1)} %get-tuple-element.15.edge_ref, ...), custom_call_target="tpu_custom_call" | custom-call | flops 4000000000 | bytes 20000000 | tf_op jit(solution)/shard_map/advance/pallas_call | solution.py:493
  (4 shorter events, 0.0 us)
Async XLA Ops:
  0.0 3.1 %copy-start = (f32[14,8,64,256]{3,2,1,0:T(8,128)S(1)}, f32[14,8,64,256]{3,2,1,0:T(8,128)}, u32[]{:S(2)}) copy-start(f32[14,8,64,256]{3,2,1,0:T(8,128)} %u_ref.5) | copy-start | bytes 22020100
  3.1 6.4 %copy-start.3 = (s32[1,1,1,128]{3,2,1,0:T(1,128)S(1)}, s32[1,1,1,128]{3,2,1,0:T(1,128)}, u32[]{:S(2)}) copy-start(s32[1,1,1,128]{3,2,1,0:T(1,128)} %param.8) | copy-start | bytes 1540
  3.1 6.4 %copy-start.1 = (f32[14,14]{1,0:T(8,128)S(1)}, f32[14,14]{1,0:T(8,128)}, u32[]{:S(2)}) copy-start(f32[14,14]{1,0:T(8,128)} %param.7) | copy-start | bytes 2356
  3.1 6.4 %copy-start.2 = (f32[14,14]{1,0:T(8,128)S(1)}, f32[14,14]{1,0:T(8,128)}, u32[]{:S(2)}) copy-start(f32[14,14]{1,0:T(8,128)} %param.6) | copy-start | bytes 2356
  3.1 9.1 %slice-start = ((s8[7340032]{0:T(1024)(128)(4,1)}), s8[4194304]{0:T(1024)(128)(4,1)S(1)}, s32[]{:S(2)}) async-start(s8[7340032]{0:T(1024)(128)(4,1)} %bitcast.10), calls=%async_computation | async-start | bytes 8388608
  3.6 20.7 %collective-permute-start.1 = (f32[3,14,8,256]{3,2,1,0:T(8,128)S(1)}, f32[3,14,8,256]{3,2,1,0:T(8,128)S(1)}, u32[]{:S(2)}, u32[]{:S(2)}) collective-permute-start(f32[3,14,8,256]{3,2,1,0:T(8,128)S(1)} %get-tuple-element.17), channel_id=1, source_target_pairs={{0,2},{2,4},{4,6},{6,0},{1,3},{3,5},{5,7},{7,1},{8,10},{10,12},{12... | collective-permute-start | bytes 1032200 | tf_op jit(solution)/shard_map/ppermute | solution.py:516
  6.7 17.7 %collective-permute-start.2 = (f32[3,14,8,256]{3,2,1,0:T(8,128)S(1)}, f32[3,14,8,256]{3,2,1,0:T(8,128)S(1)}, u32[]{:S(2)}, u32[]{:S(2)}) collective-permute-start(f32[3,14,8,256]{3,2,1,0:T(8,128)S(1)} %get-tuple-element.18), channel_id=1, source_target_pairs={{2,0},{4,2},{6,4},{0,6},{3,1},{5,3},{7,5},{1,7},{10,8},{12,10},{14... | collective-permute-start | bytes 1032200 | tf_op jit(solution)/shard_map/ppermute | solution.py:517
  9.5 2.6 %slice-start.1 = ((s8[7340032]{0:T(1024)(128)(4,1)}), s8[3145728]{0:T(1024)(128)(4,1)S(1)}, s32[]{:S(2)}) async-start(s8[7340032]{0:T(1024)(128)(4,1)} %bitcast.10), calls=%async_computation.1 | async-start | bytes 6291456
  10.5 1.6 %collective-permute-start = (f32[512,128]{1,0:T(8,128)S(1)}, f32[512,128]{1,0:T(8,128)S(1)}, u32[]{:S(2)}, u32[]{:S(2)}) collective-permute-start(f32[512,128]{1,0:T(8,128)S(1)} %pack_z.1), channel_id=1, source_target_pairs={{0,1},{1,0},{2,3},{3,2},{4,5},{5,4},{6,7},{7,6},{8,9},{9,8},{10,11... | collective-permute-start | bytes 786440 | tf_op jit(solution)/shard_map/ppermute | solution.py:115
